TPU v7x, 32 devices: a whole 2x2x4 slice. The times are simulated.
32 devices in a mesh: hst: 8 (over z, y), local: 4 (over x, core).
Axes of the slice: x: 2, y: 2, z: 4, core: 2. Of those that a mesh axis runs over, the one named last changes fastest.
Arguments:
- embedding: float32 [65536, 256], P(('hst', 'local')), may hold values from -6 to 6
- row_accum: float32 [65536], P(('hst', 'local')), may hold values from 0.5 to 8
- lookup_grads: bfloat16 [65536, 256], P(('hst', 'local')), may hold values from -3 to 3
- lookup_slot: int32 [65536], P(('hst', 'local')), may hold values from 0 to 1023, as said below
- owner_rows: int32 [32, 8, 32], P(('hst', 'local')), may hold values from -1 to 2047, as said below
Outputs:
- new_embedding: float32 [65536, 256], P(('hst', 'local'))
- new_accum: float32 [65536], P(('hst', 'local'))
- fresh_rows: bfloat16 [65536, 256], P(('hst', 'local'))
Inputs may be any that keep to these rules, and one draw needn't show every extreme that they name: For a lookup of host s, lookup_slot = o * 32 + c with owner device o and c below that host's count of live slots for o; owners with low numbers are looked up far more often. owner_rows[o, s, c] is live (not -1) exactly for c below a count of 1 to 32; every (o, s) with o mod 8 equal to s has 32 live slots; live rows of one (o, s) are distinct; a few leading slots name the same row for every host s.
All inputs are finite; a program needn't handle non-finite values.
Results may differ from a plain program's by a relative error of at most 0.0039.
Values may be sent and summed in bfloat16 or wider, within the bound.
No kernel may reach another device: no remote copies, remote signals or barrier semaphores. Data moves between devices by JAX's collectives and lax.ppermute only.
A program may use at most 64 MiB of HBM per device.

v0:
```python
import jax
import jax.numpy as jnp
from jax import lax
from jax.sharding import PartitionSpec as P


def local(embedding, row_accum, lookup_grads, lookup_slot, owner_rows):
    n_hst = lax.axis_size("hst")
    n_local = lax.axis_size("local")
    rows_dev, feat_width = embedding.shape
    capacity = owner_rows.shape[2]
    slot_count = n_hst * n_local * capacity
    onehot = (lookup_slot[:, None] == jnp.arange(slot_count, dtype=jnp.int32)[None, :]).astype(
        jnp.bfloat16
    )
    partial_value = lax.dot_general(
        onehot, lookup_grads, (((0,), (0,)), ((), ())), preferred_element_type=jnp.float32
    )
    partial_value = partial_value.astype(jnp.bfloat16).reshape(n_hst, n_local, capacity, feat_width)
    moved = lax.all_to_all(partial_value, "hst", split_axis=0, concat_axis=0, tiled=True)
    received = (
        lax.psum_scatter(moved, "local", scatter_dimension=1, tiled=True)
        .astype(jnp.float32)
        .astype(jnp.bfloat16)
    )
    received = received.astype(jnp.float32)
    row_ids = owner_rows.reshape(n_hst * capacity)
    is_live = row_ids >= 0
    target = jnp.where(is_live, row_ids, rows_dev)
    row_grad = jax.ops.segment_sum(
        received.reshape(n_hst * capacity, feat_width), target, num_segments=rows_dev + 1
    )[:rows_dev]
    new_accum = row_accum + jnp.mean(row_grad * row_grad, axis=1)
    new_embedding = embedding - 0.1 * row_grad / jnp.sqrt(new_accum)[:, None]
    safe_rows = jnp.where(is_live, row_ids, 0)
    picked = jnp.take(new_embedding, safe_rows, axis=0)
    picked = jnp.where(is_live[:, None], picked, 0.0).astype(jnp.bfloat16)
    picked = picked.reshape(n_hst, 1, capacity, feat_width)
    returned = lax.all_to_all(picked, "hst", split_axis=0, concat_axis=0, tiled=True)
    host_cache = lax.all_gather(returned, "local", axis=1, tiled=True).reshape(
        slot_count, feat_width
    )
    fresh_rows = jnp.take(host_cache, lookup_slot, axis=0)
    return (new_embedding, new_accum, fresh_rows)


def solution(mesh):
    return jax.shard_map(
        local,
        mesh=mesh,
        in_specs=(
            P(("hst", "local"), None),
            P(("hst", "local")),
            P(("hst", "local"), None),
            P(("hst", "local")),
            P(("hst", "local"), None, None),
        ),
        out_specs=(P(("hst", "local"), None), P(("hst", "local")), P(("hst", "local"), None)),
        check_vma=False,
    )
```

profile of v0, /device:TPU:0, one launch (start us, length us, event | category | flops | bytes accessed | tf_op | source)
XLA Modules:
  0.0 113.3 jit_solution(6733270233711275929)
XLA Ops:
  7.2 0.0 copy-start
  7.2 1.2 %copy-done = bf16[2048,256]{1,0:T(8,128)(2,1)S(1)} copy-done((bf16[2048,256]{1,0:T(8,128)(2,1)S(1)}, bf16[2048,256]{1,0:T(8,128)(2,1)}, u32[]{:S(2)}) %copy-start) | copy-done | bytes 1048600
  8.4 4.2 %fusion.2 = bf16[1024,256]{1,0:T(8,128)(2,1)} fusion(bf16[2048,256]{1,0:T(8,128)(2,1)S(1)} %copy-done, s32[2048]{0:T(1024)} %param.8), kind=kOutput, calls=%fused_computation.8 | convolution fusion | flops 1076101120 | bytes 1581056 | tf_op jit(solution)/shard_map/dot_general | solution.py:16
  12.6 7.3 %all-to-all-start = ((bf16[8,4,32,256]{3,2,1,0:T(8,128)(2,1)}), bf16[8,4,32,256]{3,2,1,0:T(8,128)(2,1)S(1)}, u32[]{:S(2)}, u32[]{:S(2)}) async-start(bf16[8,4,32,256]{3,2,1,0:T(8,128)(2,1)} %bitcast.1), calls=%async_computation | async-start | bytes 1048576 | tf_op jit(solution)/shard_map/all_to_all | solution.py:20
  19.9 0.0 all-reduce.3.cloned.1.call-start
  19.9 0.1 reshape.111
  20.0 14.3 %all-to-all-done = bf16[8,4,32,256]{3,2,1,0:T(8,128)(2,1)S(1)} async-done(((bf16[8,4,32,256]{3,2,1,0:T(8,128)(2,1)}), bf16[8,4,32,256]{3,2,1,0:T(8,128)(2,1)S(1)}, u32[]{:S(2)}, u32[]{:S(2)}) %all-to-all-start) | async-done | bytes 524320 | tf_op jit(solution)/shard_map/all_to_all | solution.py:20
  34.4 0.8 copy-done.2
  35.2 0.0 all-reduce.3.cloned.1.call-update
  35.2 0.6 dynamic-slice
  35.8 31.8 %all-reduce.3.cloned.1.call-done = bf16[8,4,32,256]{3,2,1,0:T(8,128)(2,1)} async-done(((bf16[8,4,32,256]{3,2,1,0:T(8,128)(2,1)}), bf16[8,4,32,256]{3,2,1,0:T(8,128)(2,1)}) %all-reduce.3.cloned.1.call-update) | async-done | bytes 524304
  67.6 1.6 %constant_dynamic-slice_fusion = bf16[8,1,32,256]{3,2,1,0:T(8,128)(2,1)S(1)} fusion(bf16[8,4,32,256]{3,2,1,0:T(8,128)(2,1)} %all-reduce.3.cloned.1.call-done, u32[]{:T(128)} %bitcast.15), kind=kLoop, calls=%fused_computation.26 | loop fusion | bytes 262148
  69.1 2.5 %scatter_custom_fusion = f32[2049,256]{1,0:T(8,128)S(1)} fusion(s32[256]{0:T(256)S(1)} %bitcast.32, f32[]{:T(128)} %constant.19.clone.1, bf16[256,256]{1,0:T(8,128)(2,1)S(1)} %bitcast.29), kind=kCustom, calls=%fused_computation.9 | custom fusion | flops 131072 | bytes 2229252 | tf_op jit(solution)/shard_map/scatter-add | solution.py:30
  71.6 0.3 multiply_reduce_fusion
  72.0 0.6 fusion.7
  72.6 0.6 copy-done.1
  73.2 1.7 %divide_subtract_fusion = f32[2048,256]{1,0:T(8,128)} fusion(f32[2048,256]{1,0:T(8,128)S(1)} %copy-done.1, f32[2049,256]{1,0:T(8,128)S(1)} %scatter_custom_fusion, f32[2048]{0:T(1024)S(1)} %get-tuple-element.3), kind=kLoop, calls=%fused_computation.6 | loop fusion | flops 1572864 | bytes 6299648 | tf_op jit(solution)/shard_map/sub | solution.py:34
  74.9 2.6 %gather_fusion = bf16[256,256]{1,0:T(8,128)(2,1)S(1)} fusion(f32[2048,256]{1,0:T(8,128)} %divide_subtract_fusion, s32[1024]{0:T(1024)S(1)} %pad_clamp_fusion), kind=kCustom, calls=%fused_computation | custom fusion | bytes 263168 | tf_op jit(solution)/shard_map/jit(_take)/gather | solution.py:36
  77.5 0.8 select_convert_fusion
  78.3 5.5 %all-to-all-start.1 = ((bf16[8,1,32,256]{3,2,1,0:T(8,128)(2,1)}), bf16[8,1,32,256]{3,2,1,0:T(8,128)(2,1)S(1)}, u32[]{:S(2)}, u32[]{:S(2)}) async-start(bf16[8,1,32,256]{3,2,1,0:T(8,128)(2,1)} %select_convert_fusion), calls=%async_computation.1 | async-start | bytes 262144 | tf_op jit(solution)/shard_map/all_to_all | solution.py:39
  83.8 7.3 %all-to-all-done.1 = bf16[8,1,32,256]{3,2,1,0:T(8,128)(2,1)S(1)} async-done(((bf16[8,1,32,256]{3,2,1,0:T(8,128)(2,1)}), bf16[8,1,32,256]{3,2,1,0:T(8,128)(2,1)S(1)}, u32[]{:S(2)}, u32[]{:S(2)}) %all-to-all-start.1) | async-done | bytes 131104 | tf_op jit(solution)/shard_map/all_to_all | solution.py:39
  91.1 6.5 %all_gather.3 = bf16[8,4,32,256]{3,2,0,1:T(8,128)(2,1)S(1)} all-gather(bf16[8,1,32,256]{3,2,0,1:T(8,128)(2,1)S(1)} %bitcast.28), channel_id=1, replica_groups=mesh['hst'=8,'local'=4] {'local'}, dimensions={1}, use_global_device_ids=true | all-gather | bytes 655360 | tf_op jit(solution)/shard_map/all_gather | solution.py:40
  97.7 7.5 %gather_fusion.1 = bf16[2048,256]{1,0:T(8,128)(2,1)S(1)} fusion(bf16[1024,256]{1,0:T(8,128)(2,1)S(1)} %bitcast.27, s32[2048]{0:T(1024)S(1)} %fusion.6), kind=kCustom, calls=%fused_computation.1 | custom fusion | bytes 2105344 | tf_op jit(solution)/shard_map/jit(_take)/gather | solution.py:43
  105.2 1.2 %broadcast_select_fusion = bf16[2048,256]{1,0:T(8,128)(2,1)} fusion(bf16[2048,256]{1,0:T(8,128)(2,1)S(1)} %gather_fusion.1, pred[2048]{0:T(1024)(128)(4,1)S(1)} %compare_and_fusion), kind=kLoop, calls=%fused_computation.11 | loop fusion | flops 524288 | bytes 2099200 | tf_op jit(solution)/shard_map/jit(_take)/select_n | solution.py:43
  (16 shorter events, 0.1 us)
Async XLA Ops:
  7.2 1.2 %copy-start = (bf16[2048,256]{1,0:T(8,128)(2,1)S(1)}, bf16[2048,256]{1,0:T(8,128)(2,1)}, u32[]{:S(2)}) copy-start(bf16[2048,256]{1,0:T(8,128)(2,1)} %param.7) | copy-start | bytes 3145732
  7.2 28.0 %copy-start.6 = (u32[32]{0:T(128)S(1)}, u32[32]{0:T(128)}, u32[]{:S(2)}) copy-start(u32[32]{0:T(128)} %constant.45) | copy-start | bytes 388
  7.2 12.7 %copy-start.4 = (s32[1,8,32]{2,1,0:T(8,128)S(1)}, s32[1,8,32]{2,1,0:T(8,128)}, u32[]{:S(2)}) copy-start(s32[1,8,32]{2,1,0:T(8,128)} %param.9) | copy-start | bytes 3076
  12.6 21.8 %all-to-all-start = ((bf16[8,4,32,256]{3,2,1,0:T(8,128)(2,1)}), bf16[8,4,32,256]{3,2,1,0:T(8,128)(2,1)S(1)}, u32[]{:S(2)}, u32[]{:S(2)}) async-start(bf16[8,4,32,256]{3,2,1,0:T(8,128)(2,1)} %bitcast.1), calls=%async_computation | async-start | bytes 1048576 | tf_op jit(solution)/shard_map/all_to_all | solution.py:20
  19.9 47.7 %all-reduce.3.cloned.1.call-start = ((), (), s32[]{:S(2)}) async-start(), calls=%async_computation.2 | async-start | bytes 1048576
  34.4 0.8 copy-start.2
  69.1 2.9 %copy-start.5 = (f32[2048]{0:T(1024)S(1)}, f32[2048]{0:T(1024)}, u32[]{:S(2)}) copy-start(f32[2048]{0:T(1024)} %param.6) | copy-start | bytes 24580
  71.6 1.6 %copy-start.1 = (f32[2048,256]{1,0:T(8,128)S(1)}, f32[2048,256]{1,0:T(8,128)}, u32[]{:S(2)}) copy-start(f32[2048,256]{1,0:T(8,128)} %param.5) | copy-start | bytes 6291460
  73.2 10.6 %copy-start.3 = (s32[2048]{0:T(1024)S(1)}, s32[2048]{0:T(1024)}, u32[]{:S(2)}) copy-start(s32[2048]{0:T(1024)} %param.8) | copy-start | bytes 24580
  78.3 12.9 %all-to-all-start.1 = ((bf16[8,1,32,256]{3,2,1,0:T(8,128)(2,1)}), bf16[8,1,32,256]{3,2,1,0:T(8,128)(2,1)S(1)}, u32[]{:S(2)}, u32[]{:S(2)}) async-start(bf16[8,1,32,256]{3,2,1,0:T(8,128)(2,1)} %select_convert_fusion), calls=%async_computation.1 | async-start | bytes 262144 | tf_op jit(solution)/shard_map/all_to_all | solution.py:39
Sparse Core Ops, SparseCore 0:
  35.3 32.2 all-reduce.2
where the time goes:
time: 114 us; the launch traced here: 113 us
  waiting for transfers between devices  53.4 us (47%)
  local copies, waits for them, and re-layouts  15 us (13%)
  between operations  14.2 us (12%)
  starting transfers between devices  12.8 us (11%)
  other arithmetic  7.17 us (6%)
  blocking collectives  6.5 us (6%)
  matrix products  4.19 us (4%)
    unnamed x2, waiting for transfers between devices  31.8 us
    all_to_all x1, waiting for transfers between devices, local(): lax.all_to_all(partial_value, 'hst', split_axis=0, concat_axis=0, tiled=T...  14.3 us
    gather x1, local copies, waits for them, and re-layouts, local(): fresh_rows = jnp.take(host_cache, lookup_slot, axis=0)  7.5 us
    all_to_all x1, waiting for transfers between devices, local(): lax.all_to_all(picked, 'hst', split_axis=0, concat_axis=0, tiled=True)  7.31 us
    all_to_all x1, starting transfers between devices, local(): lax.all_to_all(partial_value, 'hst', split_axis=0, concat_axis=0, tiled=T...  7.28 us
    all_gather x1, blocking collectives, local(): lax.all_gather(returned, 'local', axis=1, tiled=True)  6.5 us
    all_to_all x1, starting transfers between devices, local(): lax.all_to_all(picked, 'hst', split_axis=0, concat_axis=0, tiled=True)  5.51 us
    unnamed x16, local copies, waits for them, and re-layouts  4.81 us
  transfers between devices with their start and end apart: 3, of which 3 were waited for; matrix products, arithmetic and copies ran while one was open for 1% of the time, Pallas kernels for 0%

commit v1 on v0

v1 whole, which is shorter than its diff:
```python
import functools

import jax
import jax.numpy as jnp
from jax import lax
from jax.experimental import pallas as pl
from jax.experimental.pallas import tpu as pltpu
from jax.sharding import Mesh, PartitionSpec as P

MIB = 1024 * 1024


def bits_of(n):
    bits = n.bit_length() - 1
    assert n == 1 << bits
    return bits


def planes(n_hst):
    return 1 << (bits_of(n_hst) // 2)


def z_place(z, n_z, back):
    return (z - n_z // 2 if back else n_z // 2 - z) & (n_z - 1)


def member(host, chip, n_hst, chips, back):
    n_y = planes(n_hst)
    n_z = n_hst // n_y
    z, y = host // n_y, host % n_y
    return (y * chips + chip) * n_z + z_place(z, n_z, back)


def slot_place(ids, capacity, half, back):
    n_hst, chips = lax.axis_size("hst"), lax.axis_size("x")
    n_y = planes(n_hst)
    n_z = n_hst // n_y
    cap_bits, z_bits, yx_bits = bits_of(capacity), bits_of(n_z), bits_of(n_y * chips)
    other = ((ids >> cap_bits) & 1) ^ lax.axis_index("core")
    z = z_place(ids >> (cap_bits + 1 + yx_bits), n_z, back)
    yx = (ids >> (cap_bits + 1)) & ((1 << yx_bits) - 1)
    return other * half + (((yx << z_bits) + z) << cap_bits) + (ids & (capacity - 1))


def column(row):
    return jnp.transpose(jnp.broadcast_to(row, (128, 128)))


def matches(a, b):
    return jnp.where(a == b, jnp.bfloat16(1), jnp.bfloat16(0))


def small(a):
    return a.astype(jnp.int16)


def onehot_lines(place, block):
    shape = (16, place.shape[1])
    slot = small(lax.broadcasted_iota(jnp.int32, shape, 0))
    place = small(jnp.broadcast_to(place, shape))
    return jnp.concatenate(
        [matches(slot, place - jnp.int16(start)) for start in range(0, block, 16)], axis=0
    )


def load_kernel(grads_ref, out_ref, sems):
    chunks = sems.shape[0]
    piece = out_ref.shape[0] // chunks
    copies = []
    for chunk in range(chunks):
        at = pl.ds(chunk * piece, piece)
        copies.append(pltpu.make_async_copy(grads_ref.at[at], out_ref.at[at], sems.at[chunk]))
        copies[-1].start()
    for copy in copies:
        copy.wait()


def load(grads):
    return pl.pallas_call(
        load_kernel,
        in_specs=[pl.BlockSpec(memory_space=pl.ANY)],
        out_specs=pl.BlockSpec(memory_space=pltpu.VMEM),
        out_shape=jax.ShapeDtypeStruct(grads.shape, grads.dtype),
        scratch_shapes=[pltpu.SemaphoreType.DMA((16,))],
        compiler_params=pltpu.CompilerParams(vmem_limit_bytes=52 * MIB),
        cost_estimate=pl.CostEstimate(
            flops=0, bytes_accessed=4 * grads.shape[0] * grads.shape[1], transcendentals=0
        ),
        name="load",
    )(grads)


def sums_kernel(ids_ref, grads_ref, out_ref, *, base, half, capacity):
    block = out_ref.shape[0]
    place = slot_place(ids_ref[...], capacity, half, False) - (base + pl.program_id(0) * block)
    out_ref[...] = jnp.dot(
        onehot_lines(place, block), grads_ref[...], preferred_element_type=jnp.float32
    ).astype(out_ref.dtype)


def slot_sums(ids, grads, base, half, capacity):
    tokens, width = grads.shape
    block = min(512, half)
    return pl.pallas_call(
        functools.partial(sums_kernel, base=base, half=half, capacity=capacity),
        grid=(half // block,),
        in_specs=[
            pl.BlockSpec((1, tokens), lambda i: (0, 0)),
            pl.BlockSpec((tokens, width), lambda i: (0, 0)),
        ],
        out_specs=pl.BlockSpec((block, width), lambda i: (i, 0)),
        out_shape=jax.ShapeDtypeStruct((half, width), jnp.bfloat16),
        compiler_params=pltpu.CompilerParams(vmem_limit_bytes=16 * MIB),
        cost_estimate=pl.CostEstimate(
            flops=2 * half * tokens * width,
            bytes_accessed=2 * (tokens + half) * width,
            transcendentals=0,
        ),
        name="slot_sums",
    )(ids, grads)


def add_kernel(a_ref, b_ref, out_ref, lines, sems):
    chunks = sems.shape[0]
    piece = lines.shape[0] // chunks
    copies = []
    for chunk in range(chunks):
        at = slice(chunk * piece, (chunk + 1) * piece)
        total = a_ref[at, :].astype(jnp.float32) + b_ref[at, :].astype(jnp.float32)
        lines[at, :] = total.astype(jnp.bfloat16)
        window = pl.ds(chunk * piece, piece)
        copies.append(
            pltpu.make_async_copy(lines.at[window], out_ref.at[window], sems.at[chunk])
        )
        copies[-1].start()
    for copy in copies:
        copy.wait()


def add(a, b):
    vmem = pl.BlockSpec(memory_space=pltpu.VMEM)
    return pl.pallas_call(
        add_kernel,
        in_specs=[vmem] * 2,
        out_specs=pl.BlockSpec(memory_space=pl.ANY),
        out_shape=jax.ShapeDtypeStruct(a.shape, a.dtype),
        scratch_shapes=[pltpu.VMEM(a.shape, a.dtype), pltpu.SemaphoreType.DMA((4,))],
        compiler_params=pltpu.CompilerParams(vmem_limit_bytes=24 * MIB),
        cost_estimate=pl.CostEstimate(
            flops=a.size, bytes_accessed=6 * a.size, transcendentals=0
        ),
        name="add",
    )(a, b)


def prepare_kernel(
    rows_ref, emb_ref, acc_ref, ids_ref, old_ref, old_acc_ref, same_ref, cols_ref, *, half, capacity
):
    place = slot_place(ids_ref[...], capacity, half, True)
    for start in range(0, cols_ref.shape[0], 128):
        cols_ref[start : start + 128, :] = small(column(place[:, start : start + 128]))
    slots = rows_ref.shape[1]
    rows_dev = emb_ref.shape[0]
    rows = rows_ref[...]
    high = emb_ref[...].astype(jnp.bfloat16)
    low = (emb_ref[...] - high.astype(jnp.float32)).astype(jnp.bfloat16)
    row_lane = lax.broadcasted_iota(jnp.int32, (128, 128), 1)
    for start in range(0, slots, 128):
        at = slice(start, start + 128)
        col = column(rows[:, at])
        tiles = []
        acc = jnp.zeros((128, 128), jnp.float32)
        for tile in range(rows_dev // 128):
            hit = (row_lane + tile * 128) == col
            tiles.append(jnp.where(hit, 1.0, 0.0).astype(jnp.bfloat16))
            acc = acc + jnp.where(hit, acc_ref[tile : tile + 1, :], 0.0)
        onehot = jnp.concatenate(tiles, axis=1)
        old_ref[at, :] = jnp.dot(
            onehot, high, preferred_element_type=jnp.float32
        ) + jnp.dot(onehot, low, preferred_element_type=jnp.float32)
        acc = jnp.sum(acc, axis=1, keepdims=True)
        old_acc_ref[at, :] = jnp.where(col >= 0, acc, 1.0)
        for other in range(0, slots, 128):
            them = rows[:, other : other + 128]
            same_ref[at, other : other + 128] = jnp.where(
                (col == them) & (col >= 0), 1.0, 0.0
            ).astype(jnp.bfloat16)


def prepare(rows, embedding, row_accum, ids, half, capacity):
    rows_dev, width = embedding.shape
    slots = rows.shape[1]
    tokens = ids.shape[1]
    vmem = pl.BlockSpec(memory_space=pltpu.VMEM)
    return pl.pallas_call(
        functools.partial(prepare_kernel, half=half, capacity=capacity),
        in_specs=[vmem] * 4,
        out_specs=[vmem] * 4,
        out_shape=[
            jax.ShapeDtypeStruct((slots, width), jnp.float32),
            jax.ShapeDtypeStruct((slots, 128), jnp.float32),
            jax.ShapeDtypeStruct((slots, slots), jnp.bfloat16),
            jax.ShapeDtypeStruct((tokens, 128), jnp.int16),
        ],
        compiler_params=pltpu.CompilerParams(vmem_limit_bytes=24 * MIB),
        cost_estimate=pl.CostEstimate(
            flops=4 * rows_dev * slots * width,
            bytes_accessed=4 * rows_dev * width,
            transcendentals=0,
        ),
        name="prepare",
    )(rows, embedding, row_accum.reshape(rows_dev // 128, 128), ids)


def pick_kernel(arrived_ref, old_ref, acc_ref, same_ref, back_ref, sums_ref, lines, sems, *, places, back_places):
    capacity, width = arrived_ref.shape[1:]
    for host, members in enumerate(places):
        total = arrived_ref[members[0]].astype(jnp.float32)
        for place in members[1:]:
            total = total + arrived_ref[place].astype(jnp.float32)
        sums_ref[host * capacity : (host + 1) * capacity, :] = total.astype(jnp.bfloat16)
    grad = jnp.dot(same_ref[...], sums_ref[...], preferred_element_type=jnp.float32)
    square = jnp.mean(grad * grad, axis=1, keepdims=True)
    rate = 0.1 * lax.rsqrt(acc_ref[...] + square)
    for side in range(0, width, 128):
        lanes = slice(side, side + 128)
        new = (old_ref[:, lanes] - rate * grad[:, lanes]).astype(jnp.bfloat16)
        for host, members in enumerate(back_places):
            for place in members:
                lines[place, :, lanes] = new[host * capacity : (host + 1) * capacity]
    cut = lines.shape[0] // sems.shape[0]
    copies = []
    for part in range(sems.shape[0]):
        at = pl.ds(part * cut, cut)
        copies.append(pltpu.make_async_copy(lines.at[at], back_ref.at[at], sems.at[part]))
        copies[-1].start()
    for copy in copies:
        copy.wait()


def pick(arrived, old, old_acc, same, places, back_places):
    _, capacity, width = arrived.shape
    slots = len(places) * capacity
    vmem = pl.BlockSpec(memory_space=pltpu.VMEM)
    return pl.pallas_call(
        functools.partial(pick_kernel, places=places, back_places=back_places),
        in_specs=[vmem] * 4,
        out_specs=[pl.BlockSpec(memory_space=pl.ANY), vmem],
        out_shape=[
            jax.ShapeDtypeStruct(arrived.shape, jnp.bfloat16),
            jax.ShapeDtypeStruct((slots, width), jnp.bfloat16),
        ],
        scratch_shapes=[
            pltpu.VMEM(arrived.shape, jnp.bfloat16),
            pltpu.SemaphoreType.DMA((2,)),
        ],
        compiler_params=pltpu.CompilerParams(vmem_limit_bytes=24 * MIB),
        cost_estimate=pl.CostEstimate(
            flops=2 * slots * slots * width,
            bytes_accessed=8 * slots * width,
            transcendentals=slots,
        ),
        name="pick",
    )(arrived, old, old_acc, same)


def update_kernel(rows_ref, sums_ref, emb_ref, acc_ref, new_emb_ref, new_acc_ref):
    block, width = emb_ref.shape
    onehot = onehot_lines(rows_ref[...] - pl.program_id(0) * block, block)
    grad = jnp.dot(onehot, sums_ref[...], preferred_element_type=jnp.float32)
    square = jnp.mean(grad * grad, axis=1, keepdims=True)
    diagonal = lax.broadcasted_iota(jnp.int32, (128, 128), 0) == lax.broadcasted_iota(
        jnp.int32, (128, 128), 1
    )
    for part in range(block // 128):
        at = slice(part * 128, part * 128 + 128)
        acc = column(acc_ref[0, part : part + 1, :]) + square[at]
        new_acc_ref[0, part : part + 1, :] = jnp.sum(
            jnp.where(diagonal, acc, 0.0), axis=0, keepdims=True
        )
        rate = 0.1 * lax.rsqrt(acc)
        for side in range(0, width, 128):
            lanes = slice(side, side + 128)
            new_emb_ref[at, lanes] = emb_ref[at, lanes] - rate * grad[at, lanes]


def update(rows, sums, embedding, row_accum):
    rows_dev, width = embedding.shape
    slots = rows.shape[1]
    block = 512
    steps = rows_dev // block
    accum = row_accum.reshape(steps, block // 128, 128)
    table = pl.BlockSpec((block, width), lambda i: (i, 0))
    line = pl.BlockSpec((1, block // 128, 128), lambda i: (i, 0, 0))
    new_emb, new_acc = pl.pallas_call(
        update_kernel,
        grid=(steps,),
        in_specs=[
            pl.BlockSpec((1, slots), lambda i: (0, 0)),
            pl.BlockSpec((slots, width), lambda i: (0, 0)),
            table,
            line,
        ],
        out_specs=[table, line],
        out_shape=[
            jax.ShapeDtypeStruct((rows_dev, width), jnp.float32),
            jax.ShapeDtypeStruct(accum.shape, jnp.float32),
        ],
        compiler_params=pltpu.CompilerParams(vmem_limit_bytes=16 * MIB),
        cost_estimate=pl.CostEstimate(
            flops=2 * rows_dev * slots * width,
            bytes_accessed=8 * rows_dev * width,
            transcendentals=rows_dev,
        ),
        name="update",
    )(rows, sums, embedding, accum)
    return new_emb, new_acc.reshape(rows_dev)


def chosen_rows(cols, cache, base):
    slots = cache.shape[0]
    lane = lax.broadcasted_iota(jnp.int32, cols.shape, 1)
    onehot = jnp.concatenate(
        [matches(cols, small(lane + (base + start))) for start in range(0, slots, 128)], axis=1
    )
    return jnp.dot(onehot, cache, preferred_element_type=jnp.float32)


def first_expand_kernel(cols_ref, cache_ref, out_ref):
    block = min(1024, MIB // cache_ref.shape[0])
    for start in range(0, out_ref.shape[0], block):
        at = slice(start, start + block)
        out_ref[at, :] = chosen_rows(cols_ref[at, :], cache_ref[...], 0).astype(jnp.bfloat16)


def second_expand_kernel(cols_ref, cache_ref, before_ref, out_ref, lines, sems):
    block = lines.shape[0] // sems.shape[0]
    copies = []
    for start in range(0, lines.shape[0], block):
        at = slice(start, start + block)
        rows = chosen_rows(cols_ref[at, :], cache_ref[...], cache_ref.shape[0])
        lines[at, :] = (rows + before_ref[at, :].astype(jnp.float32)).astype(jnp.bfloat16)
        window = pl.ds(start, block)
        copies.append(
            pltpu.make_async_copy(lines.at[window], out_ref.at[window], sems.at[start // block])
        )
        copies[-1].start()
    for copy in copies:
        copy.wait()


def expand(cols, cache, before=None):
    slots, width = cache.shape
    tokens = cols.shape[0]
    vmem = pl.BlockSpec(memory_space=pltpu.VMEM)
    last = before is not None
    return pl.pallas_call(
        second_expand_kernel if last else first_expand_kernel,
        in_specs=[vmem] * (2 + last),
        out_specs=pl.BlockSpec(memory_space=pltpu.HBM) if last else vmem,
        out_shape=jax.ShapeDtypeStruct((tokens, width), jnp.bfloat16),
        scratch_shapes=[
            pltpu.VMEM((tokens, width), jnp.bfloat16),
            pltpu.SemaphoreType.DMA((tokens // 256,)),
        ]
        if last
        else [],
        compiler_params=pltpu.CompilerParams(vmem_limit_bytes=32 * MIB),
        cost_estimate=pl.CostEstimate(
            flops=2 * slots * tokens * width,
            bytes_accessed=2 * (tokens + slots) * width,
            transcendentals=0,
        ),
        name="second_expand" if last else "first_expand",
    )(cols, cache, *([before] if last else []))


def local(embedding, row_accum, lookup_grads, lookup_slot, owner_rows):
    n_hst = lax.axis_size("hst")
    chips = lax.axis_size("x")
    width = embedding.shape[1]
    capacity = owner_rows.shape[2]
    half = n_hst * chips * capacity

    def swap(block):
        return lax.ppermute(block, "core", [(0, 1), (1, 0)])

    members = n_hst * chips

    def places(back):
        return [[member(h, x, n_hst, chips, back) for x in range(chips)] for h in range(n_hst)]

    def exchange(blocks, back):
        order = [0] * members
        for host, row in enumerate(places(back)):
            for chip, place in enumerate(row):
                order[place] = host * chips + chip
        blocks = blocks.reshape(members, capacity, width)
        return lax.all_to_all(
            blocks, ("hst", "x"), split_axis=0, concat_axis=0, axis_index_groups=[order], tiled=True
        )

    rows = owner_rows.reshape(1, n_hst * capacity)
    ids = lookup_slot.reshape(1, -1)
    grads = load(lookup_grads)
    arrived = swap(slot_sums(ids, grads, half, half, capacity))
    kept = slot_sums(ids, grads, 0, half, capacity)
    arrived = exchange(add(kept, arrived), False)
    old, old_acc, same, cols = prepare(rows, embedding, row_accum, ids, half, capacity)
    back, sums = pick(arrived, old, old_acc, same, places(False), places(True))
    cache = exchange(back, True).reshape(half, width)
    new_embedding, new_accum = update(rows, sums, embedding, row_accum)
    cache, new_embedding, new_accum = lax.optimization_barrier((cache, new_embedding, new_accum))

    other = swap(cache)
    fresh_rows = expand(cols, cache)
    fresh_rows = expand(cols, other, fresh_rows)
    return (new_embedding, new_accum, fresh_rows)


def solution(mesh):
    chips = mesh.shape["local"] // 2
    fine = Mesh(mesh.devices.reshape(mesh.shape["hst"], chips, 2), ("hst", "x", "core"))
    whole = ("hst", "x", "core")
    return jax.shard_map(
        local,
        mesh=fine,
        in_specs=(P(whole, None), P(whole), P(whole, None), P(whole), P(whole, None, None)),
        out_specs=(P(whole, None), P(whole), P(whole, None)),
        check_vma=False,
    )
```

time: 114 us -> 37.5 us (0.33)
  waiting for transfers between devices: 53.4 us -> 10.3 us
  local copies, waits for them, and re-layouts: 15 us -> 0.1 us
  between operations: 14.2 us -> 0.73 us
  Pallas kernels: 0 us -> 10.6 us
  other arithmetic: 7.17 us -> 0 us
  blocking collectives: 6.5 us -> 0 us
  matrix products: 4.19 us -> 0 us
  starting transfers between devices: 12.8 us -> 15.4 us
    unnamed x2 -> x0, waiting for transfers between devices: 31.8 us -> none
    all_to_all x2, waiting for transfers between devices: 21.7 us -> 8.99 us  [exchange(): lax.all_to_all(blocks, ('hst', 'x'), split_axis=0, concat_axis=0, axis_in...]
    pallas_call x0 -> x9, Pallas kernels: none -> 10.6 us  [the longest x1 2.75 us: update(): pl.pallas_call(update_kernel, grid=(steps,), in_specs=[pl.BlockSpec((1, s...]
    gather x2 -> x0, local copies, waits for them, and re-layouts: 10.1 us -> none  [the longest x1 7.5 us: local(): fresh_rows = jnp.take(host_cache, lookup_slot, axis=0)]
    all_gather x1 -> x0, blocking collectives: 6.5 us -> none  [local(): lax.all_gather(returned, 'local', axis=1, tiled=True)]
    unnamed x16 -> x8, local copies, waits for them, and re-layouts: 4.81 us -> 0.02 us
    dot_general x1 -> x0, matrix products: 4.19 us -> none  [local(): lax.dot_general(onehot, lookup_grads, (((0,), (0,)), ((), ())), preferred...]
    scatter-add x1 -> x0, other arithmetic: 2.48 us -> none  [local(): jax.ops.segment_sum(received.reshape(n_hst * capacity, feat_width), targe...]
  transfers between devices with their start and end apart: 3 -> 4, of which waited for: 3 -> 4; matrix products, arithmetic and copies ran while one was open for 1% -> 0% of each run, Pallas kernels for 0% -> 14%
where the time goes in v1:
time: 37.5 us; the launch traced here: 37.1 us
  starting transfers between devices  15.4 us (41%)
  Pallas kernels  10.6 us (28%)
  waiting for transfers between devices  10.3 us (27%)
  between operations  0.73 us (2%)
    all_to_all x2, starting transfers between devices, exchange(): lax.all_to_all(blocks, ('hst', 'x'), split_axis=0, concat_axis=0, axis_in...  14.9 us
    all_to_all x2, waiting for transfers between devices, exchange(): lax.all_to_all(blocks, ('hst', 'x'), split_axis=0, concat_axis=0, axis_in...  8.99 us
    pallas_call x1, Pallas kernels, update(): pl.pallas_call(update_kernel, grid=(steps,), in_specs=[pl.BlockSpec((1, s...  2.75 us
    pallas_call x2, Pallas kernels, expand(): pl.pallas_call(second_expand_kernel if last else first_expand_kernel, in_...  2.23 us
    pallas_call x2, Pallas kernels, slot_sums(): pl.pallas_call(functools.partial(sums_kernel, base=base, half=half, capac...  1.42 us
    pallas_call x1, Pallas kernels, load(): pl.pallas_call(load_kernel, in_specs=[pl.BlockSpec(memory_space=pl.ANY)],...  1.38 us
    ppermute x2, waiting for transfers between devices, swap(): return lax.ppermute(block, 'core', [(0, 1), (1, 0)])  1.27 us
    pallas_call x1, Pallas kernels, prepare(): pl.pallas_call(functools.partial(prepare_kernel, half=half, capacity=capa...  1.07 us
  transfers between devices with their start and end apart: 4, of which 4 were waited for; matrix products, arithmetic and copies ran while one was open for 0% of the time, Pallas kernels for 14%

profile of v1, /device:TPU:0, one launch (start us, length us, event | category | flops | bytes accessed | tf_op | source)
XLA Modules:
  0.0 37.1 jit_solution(11024350033440621163)
XLA Ops:
  0.6 0.0 copy-start.2
  0.6 1.4 %load.1.grads_ref = bf16[2048,256]{1,0:T(8,128)(2,1)S(1)} custom-call(bf16[2048,256]{1,0:T(8,128)(2,1)} %grads_ref.1), custom_call_target="tpu_custom_call" | custom-call | bytes 2097152 | tf_op jit(solution)/shard_map/load/pallas_call | solution.py:79
  2.0 0.0 copy-done.2
  2.0 0.7 %slot_sums.3 = bf16[512,256]{1,0:T(8,128)(2,1)S(1)} custom-call(s32[1,2048]{1,0:T(1,128)S(1)} %bitcast.10, bf16[2048,256]{1,0:T(8,128)(2,1)S(1)} %load.1.grads_ref), custom_call_target="tpu_custom_call" | custom-call | flops 536870912 | bytes 1310720 | tf_op jit(solution)/shard_map/slot_sums/pallas_call | solution.py:104
  2.8 0.0 copy-start.3
  2.8 0.0 copy-start
  2.8 0.0 copy-start.1
  2.8 0.5 %collective-permute-start = (bf16[512,256]{1,0:T(8,128)(2,1)S(1)}, bf16[512,256]{1,0:T(8,128)(2,1)S(1)}, u32[]{:S(2)}, u32[]{:S(2)}) collective-permute-start(bf16[512,256]{1,0:T(8,128)(2,1)S(1)} %slot_sums.3), channel_id=1, source_target_pairs={{0,1},{1,0},{2,3},{3,2},{4,5},{5,4},{6,7},{7,6},{8,9},{9,8},{10,11... | collective-permute-start | bytes 786440 | tf_op jit(solution)/shard_map/ppermute | solution.py:386
  3.3 0.7 %slot_sums.2.a_ref = bf16[512,256]{1,0:T(8,128)(2,1)S(1)} custom-call(s32[1,2048]{1,0:T(1,128)S(1)} %bitcast.11, bf16[2048,256]{1,0:T(8,128)(2,1)S(1)} %load.1.grads_ref), custom_call_target="tpu_custom_call" | custom-call | flops 536870912 | bytes 1310720 | tf_op jit(solution)/shard_map/slot_sums/pallas_call | solution.py:104
  4.0 0.4 %collective-permute-done.b_ref = bf16[512,256]{1,0:T(8,128)(2,1)S(1)} collective-permute-done((bf16[512,256]{1,0:T(8,128)(2,1)S(1)}, bf16[512,256]{1,0:T(8,128)(2,1)S(1)}, u32[]{:S(2)}, u32[]{:S(2)}) %collective-permute-start) | collective-permute-done | bytes 262176 | tf_op jit(solution)/shard_map/ppermute | solution.py:386
  4.5 0.7 %add.1 = bf16[512,256]{1,0:T(8,128)(2,1)} custom-call(bf16[512,256]{1,0:T(8,128)(2,1)S(1)} %slot_sums.2.a_ref, bf16[512,256]{1,0:T(8,128)(2,1)S(1)} %collective-permute-done.b_ref), custom_call_target="tpu_custom_call" | custom-call | flops 131072 | bytes 786432 | tf_op jit(solution)/shard_map/add/pallas_call | solution.py:142
  5.2 8.7 %all-to-all-start = ((bf16[16,32,256]{2,1,0:T(8,128)(2,1)}), bf16[16,32,256]{2,1,0:T(8,128)(2,1)S(1)}, u32[]{:S(2)}, u32[]{:S(2)}) async-start(bf16[16,32,256]{2,1,0:T(8,128)(2,1)} %bitcast.1), calls=%async_computation | async-start | bytes 524288 | tf_op jit(solution)/shard_map/all_to_all | solution.py:399
  13.9 0.0 copy-done.3
  13.9 0.1 reshape.29.rows_ref
  14.0 1.1 %prepare.1 = (f32[256,256]{1,0:T(8,128)S(1)}, f32[256,128]{1,0:T(8,128)S(1)}, bf16[256,256]{1,0:T(8,128)(2,1)S(1)}, s16[2048,128]{1,0:T(8,128)(2,1)S(1)}) custom-call(s32[1,256]{1,0:T(1,128)S(1)} %reshape.29.rows_ref, f32[2048,256]{1,0:T(8,128)S(1)} %copy-done, f32[16,128]{1,0:T(8,128)S(1)} %bitcast.8, s32[1,2048]{1,0:T(1,128)S(1)} %bitcast.12), custom_call_target="tpu_custom_call" | custom-call | flops 536870912 | bytes 2097152 | tf_op jit(solution)/shard_map/prepare/pallas_call | solution.py:195
  15.1 5.6 %all-to-all-done.arrived_ref = bf16[16,32,256]{2,1,0:T(8,128)(2,1)S(1)} async-done(((bf16[16,32,256]{2,1,0:T(8,128)(2,1)}), bf16[16,32,256]{2,1,0:T(8,128)(2,1)S(1)}, u32[]{:S(2)}, u32[]{:S(2)}) %all-to-all-start) | async-done | bytes 262176 | tf_op jit(solution)/shard_map/all_to_all | solution.py:399
  20.7 1.0 %pick.1 = (bf16[16,32,256]{2,1,0:T(8,128)(2,1)}, bf16[256,256]{1,0:T(8,128)(2,1)S(1)}) custom-call(bf16[16,32,256]{2,1,0:T(8,128)(2,1)S(1)} %all-to-all-done.arrived_ref, f32[256,256]{1,0:T(8,128)S(1)} %get-tuple-element.14.old_ref, f32[256,128]{1,0:T(8,128)S(1)} %get-tuple-element.15.acc_ref, bf16[256,256]{1,0:T(8,128)(2,1)S(1)} %get-tuple-element.16.same_ref), custom_call_target="tpu_custom_call" | custom-call | flops 33554432 | bytes 524288 | tf_op jit(solution)/shard_map/pick/pallas_call | solution.py:245
  21.7 6.1 %all-to-all-start.1 = ((bf16[16,32,256]{2,1,0:T(8,128)(2,1)}), bf16[16,32,256]{2,1,0:T(8,128)(2,1)S(1)}, u32[]{:S(2)}, u32[]{:S(2)}) async-start(bf16[16,32,256]{2,1,0:T(8,128)(2,1)} %get-tuple-element.17), calls=%async_computation.1 | async-start | bytes 524288 | tf_op jit(solution)/shard_map/all_to_all | solution.py:399
  27.9 2.8 %update.1 = (f32[2048,256]{1,0:T(8,128)}, f32[4,4,128]{2,1,0:T(4,128)}) custom-call(s32[1,256]{1,0:T(1,128)S(1)} %reshape.29.rows_ref, bf16[256,256]{1,0:T(8,128)(2,1)S(1)} %get-tuple-element.18.sums_ref, f32[2048,256]{1,0:T(8,128)S(1)} %copy-done, f32[4,4,128]{2,1,0:T(4,128)S(1)} %bitcast.9), custom_call_target="tpu_custom_call" | custom-call | flops 268435456 | bytes 4194304 | tf_op jit(solution)/shard_map/update/pallas_call | solution.py:295
  30.6 3.4 %all-to-all-done.1 = bf16[16,32,256]{2,1,0:T(8,128)(2,1)S(1)} async-done(((bf16[16,32,256]{2,1,0:T(8,128)(2,1)}), bf16[16,32,256]{2,1,0:T(8,128)(2,1)S(1)}, u32[]{:S(2)}, u32[]{:S(2)}) %all-to-all-start.1) | async-done | bytes 262176 | tf_op jit(solution)/shard_map/all_to_all | solution.py:399
  34.0 0.0 collective-permute-start.1
  34.0 0.7 %first_expand.1.before_ref = bf16[2048,256]{1,0:T(8,128)(2,1)S(1)} custom-call(s16[2048,128]{1,0:T(8,128)(2,1)S(1)} %get-tuple-element.23.cols_ref, bf16[512,256]{1,0:T(8,128)(2,1)S(1)} %bitcast.7), custom_call_target="tpu_custom_call" | custom-call | flops 536870912 | bytes 1310720 | tf_op jit(solution)/shard_map/first_expand/pallas_call | solution.py:357
  34.7 0.8 %collective-permute-done.1.cache_ref = bf16[512,256]{1,0:T(8,128)(2,1)S(1)} collective-permute-done((bf16[512,256]{1,0:T(8,128)(2,1)S(1)}, bf16[512,256]{1,0:T(8,128)(2,1)S(1)}, u32[]{:S(2)}, u32[]{:S(2)}) %collective-permute-start.1) | collective-permute-done | bytes 262176 | tf_op jit(solution)/shard_map/ppermute | solution.py:386
  35.5 1.5 %second_expand.1 = bf16[2048,256]{1,0:T(8,128)(2,1)} custom-call(s16[2048,128]{1,0:T(8,128)(2,1)S(1)} %get-tuple-element.23.cols_ref, bf16[512,256]{1,0:T(8,128)(2,1)S(1)} %collective-permute-done.1.cache_ref, bf16[2048,256]{1,0:T(8,128)(2,1)S(1)} %first_expand.1.before_ref), custom_call_target="tpu_custom_call" | custom-call | flops 536870912 | bytes 1310720 | tf_op jit(solution)/shard_map/second_expand/pallas_call | solution.py:357
  (2 shorter events, 0.0 us)
Async XLA Ops:
  0.6 1.4 %copy-start.2 = (s32[2048]{0:T(1024)S(1)}, s32[2048]{0:T(1024)}, u32[]{:S(2)}) copy-start(s32[2048]{0:T(1024)} %param.8) | copy-start | bytes 24580
  2.8 11.2 %copy-start.3 = (s32[1,8,32]{2,1,0:T(8,128)S(1)}, s32[1,8,32]{2,1,0:T(8,128)}, u32[]{:S(2)}) copy-start(s32[1,8,32]{2,1,0:T(8,128)} %param.9) | copy-start | bytes 3076
  2.8 11.3 %copy-start = (f32[2048,256]{1,0:T(8,128)S(1)}, f32[2048,256]{1,0:T(8,128)}, u32[]{:S(2)}) copy-start(f32[2048,256]{1,0:T(8,128)} %emb_ref.3) | copy-start | bytes 6291460
  2.8 11.3 %copy-start.1 = (f32[2048]{0:T(1024)S(1)}, f32[2048]{0:T(1024)}, u32[]{:S(2)}) copy-start(f32[2048]{0:T(1024)} %param.6) | copy-start | bytes 24580
  2.8 1.7 %collective-permute-start = (bf16[512,256]{1,0:T(8,128)(2,1)S(1)}, bf16[512,256]{1,0:T(8,128)(2,1)S(1)}, u32[]{:S(2)}, u32[]{:S(2)}) collective-permute-start(bf16[512,256]{1,0:T(8,128)(2,1)S(1)} %slot_sums.3), channel_id=1, source_target_pairs={{0,1},{1,0},{2,3},{3,2},{4,5},{5,4},{6,7},{7,6},{8,9},{9,8},{10,11... | collective-permute-start | bytes 786440 | tf_op jit(solution)/shard_map/ppermute | solution.py:386
  5.2 15.5 %all-to-all-start = ((bf16[16,32,256]{2,1,0:T(8,128)(2,1)}), bf16[16,32,256]{2,1,0:T(8,128)(2,1)S(1)}, u32[]{:S(2)}, u32[]{:S(2)}) async-start(bf16[16,32,256]{2,1,0:T(8,128)(2,1)} %bitcast.1), calls=%async_computation | async-start | bytes 524288 | tf_op jit(solution)/shard_map/all_to_all | solution.py:399
  21.7 12.3 %all-to-all-start.1 = ((bf16[16,32,256]{2,1,0:T(8,128)(2,1)}), bf16[16,32,256]{2,1,0:T(8,128)(2,1)S(1)}, u32[]{:S(2)}, u32[]{:S(2)}) async-start(bf16[16,32,256]{2,1,0:T(8,128)(2,1)} %get-tuple-element.17), calls=%async_computation.1 | async-start | bytes 524288 | tf_op jit(solution)/shard_map/all_to_all | solution.py:399
  34.0 1.5 %collective-permute-start.1 = (bf16[512,256]{1,0:T(8,128)(2,1)S(1)}, bf16[512,256]{1,0:T(8,128)(2,1)S(1)}, u32[]{:S(2)}, u32[]{:S(2)}) collective-permute-start(bf16[512,256]{1,0:T(8,128)(2,1)S(1)} %bitcast.6), channel_id=1, source_target_pairs={{0,1},{1,0},{2,3},{3,2},{4,5},{5,4},{6,7},{7,6},{8,9},{9,8},{10,11... | collective-permute-start | bytes 786440 | tf_op jit(solution)/shard_map/ppermute | solution.py:386

commit v2 on v1

--- a/solution.py
+++ b/solution.py
@@ -20,26 +20,25 @@
     return 1 << (bits_of(n_hst) // 2)
 
 
-def z_place(z, n_z, back):
-    return (z - n_z // 2 if back else n_z // 2 - z) & (n_z - 1)
-
-
-def member(host, chip, n_hst, chips, back):
+def chip_order(n_hst, chips, back):
     n_y = planes(n_hst)
-    n_z = n_hst // n_y
-    z, y = host // n_y, host % n_y
-    return (y * chips + chip) * n_z + z_place(z, n_z, back)
+    n_z, n_yx = n_hst // n_y, n_y * chips
+    mid = n_z // 2
+    if back:
+        zs = [*range(mid, n_z), *reversed(range(mid))]
+        return [z * n_yx + yx for z in zs for yx in reversed(range(n_yx))]
+    zs = [*reversed(range(mid + 1)), *reversed(range(mid + 1, n_z))]
+    return [z * n_yx + (at ^ (n_yx // 2)) for at in range(n_yx) for z in zs]
 
 
 def slot_place(ids, capacity, half, back):
-    n_hst, chips = lax.axis_size("hst"), lax.axis_size("x")
-    n_y = planes(n_hst)
-    n_z = n_hst // n_y
-    cap_bits, z_bits, yx_bits = bits_of(capacity), bits_of(n_z), bits_of(n_y * chips)
+    cap_bits = bits_of(capacity)
     other = ((ids >> cap_bits) & 1) ^ lax.axis_index("core")
-    z = z_place(ids >> (cap_bits + 1 + yx_bits), n_z, back)
-    yx = (ids >> (cap_bits + 1)) & ((1 << yx_bits) - 1)
-    return other * half + (((yx << z_bits) + z) << cap_bits) + (ids & (capacity - 1))
+    chip = ids >> (cap_bits + 1)
+    place = jnp.zeros_like(chip)
+    for at, member in enumerate(chip_order(lax.axis_size("hst"), lax.axis_size("x"), back)):
+        place = jnp.where(chip == member, at, place)
+    return other * half + (place << cap_bits) + (ids & (capacity - 1))
 
 
 def column(row):
@@ -81,7 +80,7 @@
         in_specs=[pl.BlockSpec(memory_space=pl.ANY)],
         out_specs=pl.BlockSpec(memory_space=pltpu.VMEM),
         out_shape=jax.ShapeDtypeStruct(grads.shape, grads.dtype),
-        scratch_shapes=[pltpu.SemaphoreType.DMA((16,))],
+        scratch_shapes=[pltpu.SemaphoreType.DMA((2,))],
         compiler_params=pltpu.CompilerParams(vmem_limit_bytes=52 * MIB),
         cost_estimate=pl.CostEstimate(
             flops=0, bytes_accessed=4 * grads.shape[0] * grads.shape[1], transcendentals=0
@@ -388,13 +387,11 @@
     members = n_hst * chips
 
     def places(back):
-        return [[member(h, x, n_hst, chips, back) for x in range(chips)] for h in range(n_hst)]
+        order = chip_order(n_hst, chips, back)
+        return [[order.index(h * chips + x) for x in range(chips)] for h in range(n_hst)]
 
     def exchange(blocks, back):
-        order = [0] * members
-        for host, row in enumerate(places(back)):
-            for chip, place in enumerate(row):
-                order[place] = host * chips + chip
+        order = chip_order(n_hst, chips, back)
         blocks = blocks.reshape(members, capacity, width)
         return lax.all_to_all(
             blocks, ("hst", "x"), split_axis=0, concat_axis=0, axis_index_groups=[order], tiled=True

time: 37.5 us -> 36.4 us (0.971)
  waiting for transfers between devices: 10.3 us -> 9.1 us
    all_to_all x2, waiting for transfers between devices: 8.99 us -> 7.83 us  [exchange(): lax.all_to_all(blocks, ('hst', 'x'), split_axis=0, concat_axis=0, axis_in...]
  transfers between devices with their start and end apart: 4 -> 4, of which waited for: 4 -> 4; matrix products, arithmetic and copies ran while one was open for 0% -> 0% of each run, Pallas kernels for 14% -> 15%
where the time goes in v2:
time: 36.4 us; the launch traced here: 36 us
  starting transfers between devices  15.6 us (43%)
  Pallas kernels  10.5 us (29%)
  waiting for transfers between devices  9.1 us (25%)
  between operations  0.73 us (2%)
    all_to_all x2, starting transfers between devices, exchange(): lax.all_to_all(blocks, ('hst', 'x'), split_axis=0, concat_axis=0, axis_in...  15.1 us
    all_to_all x2, waiting for transfers between devices, exchange(): lax.all_to_all(blocks, ('hst', 'x'), split_axis=0, concat_axis=0, axis_in...  7.83 us
    pallas_call x1, Pallas kernels, update(): pl.pallas_call(update_kernel, grid=(steps,), in_specs=[pl.BlockSpec((1, s...  2.75 us
    pallas_call x2, Pallas kernels, expand(): pl.pallas_call(second_expand_kernel if last else first_expand_kernel, in_...  2.23 us
    pallas_call x2, Pallas kernels, slot_sums(): pl.pallas_call(functools.partial(sums_kernel, base=base, half=half, capac...  1.41 us
    ppermute x2, waiting for transfers between devices, swap(): return lax.ppermute(block, 'core', [(0, 1), (1, 0)])  1.27 us
    pallas_call x1, Pallas kernels, load(): pl.pallas_call(load_kernel, in_specs=[pl.BlockSpec(memory_space=pl.ANY)],...  1.22 us
    pallas_call x1, Pallas kernels, prepare(): pl.pallas_call(functools.partial(prepare_kernel, half=half, capacity=capa...  1.08 us
  transfers between devices with their start and end apart: 4, of which 4 were waited for; matrix products, arithmetic and copies ran while one was open for 0% of the time, Pallas kernels for 15%

profile of v2, /device:TPU:0, one launch (start us, length us, event | category | flops | bytes accessed | tf_op | source)
XLA Modules:
  0.0 36.0 jit_solution(16818217984157819333)
XLA Ops:
  0.6 0.0 copy-start.2
  0.6 1.2 %load.1.grads_ref = bf16[2048,256]{1,0:T(8,128)(2,1)S(1)} custom-call(bf16[2048,256]{1,0:T(8,128)(2,1)} %grads_ref.1), custom_call_target="tpu_custom_call" | custom-call | bytes 2097152 | tf_op jit(solution)/shard_map/load/pallas_call | solution.py:78
  1.9 0.0 copy-done.2
  1.9 0.7 %slot_sums.3 = bf16[512,256]{1,0:T(8,128)(2,1)S(1)} custom-call(s32[1,2048]{1,0:T(1,128)S(1)} %bitcast.10, bf16[2048,256]{1,0:T(8,128)(2,1)S(1)} %load.1.grads_ref), custom_call_target="tpu_custom_call" | custom-call | flops 536870912 | bytes 1310720 | tf_op jit(solution)/shard_map/slot_sums/pallas_call | solution.py:103
  2.6 0.0 copy-start.3
  2.6 0.0 copy-start
  2.6 0.0 copy-start.1
  2.6 0.5 %collective-permute-start = (bf16[512,256]{1,0:T(8,128)(2,1)S(1)}, bf16[512,256]{1,0:T(8,128)(2,1)S(1)}, u32[]{:S(2)}, u32[]{:S(2)}) collective-permute-start(bf16[512,256]{1,0:T(8,128)(2,1)S(1)} %slot_sums.3), channel_id=1, source_target_pairs={{0,1},{1,0},{2,3},{3,2},{4,5},{5,4},{6,7},{7,6},{8,9},{9,8},{10,11... | collective-permute-start | bytes 786440 | tf_op jit(solution)/shard_map/ppermute | solution.py:385
  3.1 0.7 %slot_sums.2.a_ref = bf16[512,256]{1,0:T(8,128)(2,1)S(1)} custom-call(s32[1,2048]{1,0:T(1,128)S(1)} %bitcast.11, bf16[2048,256]{1,0:T(8,128)(2,1)S(1)} %load.1.grads_ref), custom_call_target="tpu_custom_call" | custom-call | flops 536870912 | bytes 1310720 | tf_op jit(solution)/shard_map/slot_sums/pallas_call | solution.py:103
  3.9 0.5 %collective-permute-done.b_ref = bf16[512,256]{1,0:T(8,128)(2,1)S(1)} collective-permute-done((bf16[512,256]{1,0:T(8,128)(2,1)S(1)}, bf16[512,256]{1,0:T(8,128)(2,1)S(1)}, u32[]{:S(2)}, u32[]{:S(2)}) %collective-permute-start) | collective-permute-done | bytes 262176 | tf_op jit(solution)/shard_map/ppermute | solution.py:385
  4.3 0.7 %add.1 = bf16[512,256]{1,0:T(8,128)(2,1)} custom-call(bf16[512,256]{1,0:T(8,128)(2,1)S(1)} %slot_sums.2.a_ref, bf16[512,256]{1,0:T(8,128)(2,1)S(1)} %collective-permute-done.b_ref), custom_call_target="tpu_custom_call" | custom-call | flops 131072 | bytes 786432 | tf_op jit(solution)/shard_map/add/pallas_call | solution.py:141
  5.1 8.7 %all-to-all-start = ((bf16[16,32,256]{2,1,0:T(8,128)(2,1)}), bf16[16,32,256]{2,1,0:T(8,128)(2,1)S(1)}, u32[]{:S(2)}, u32[]{:S(2)}) async-start(bf16[16,32,256]{2,1,0:T(8,128)(2,1)} %bitcast.1), calls=%async_computation | async-start | bytes 524288 | tf_op jit(solution)/shard_map/all_to_all | solution.py:396
  13.8 0.0 copy-done.3
  13.8 0.1 reshape.29.rows_ref
  13.9 1.1 %prepare.1 = (f32[256,256]{1,0:T(8,128)S(1)}, f32[256,128]{1,0:T(8,128)S(1)}, bf16[256,256]{1,0:T(8,128)(2,1)S(1)}, s16[2048,128]{1,0:T(8,128)(2,1)S(1)}) custom-call(s32[1,256]{1,0:T(1,128)S(1)} %reshape.29.rows_ref, f32[2048,256]{1,0:T(8,128)S(1)} %copy-done, f32[16,128]{1,0:T(8,128)S(1)} %bitcast.8, s32[1,2048]{1,0:T(1,128)S(1)} %bitcast.12), custom_call_target="tpu_custom_call" | custom-call | flops 536870912 | bytes 2097152 | tf_op jit(solution)/shard_map/prepare/pallas_call | solution.py:194
  15.0 5.6 %all-to-all-done.arrived_ref = bf16[16,32,256]{2,1,0:T(8,128)(2,1)S(1)} async-done(((bf16[16,32,256]{2,1,0:T(8,128)(2,1)}), bf16[16,32,256]{2,1,0:T(8,128)(2,1)S(1)}, u32[]{:S(2)}, u32[]{:S(2)}) %all-to-all-start) | async-done | bytes 262176 | tf_op jit(solution)/shard_map/all_to_all | solution.py:396
  20.6 1.0 %pick.1 = (bf16[16,32,256]{2,1,0:T(8,128)(2,1)}, bf16[256,256]{1,0:T(8,128)(2,1)S(1)}) custom-call(bf16[16,32,256]{2,1,0:T(8,128)(2,1)S(1)} %all-to-all-done.arrived_ref, f32[256,256]{1,0:T(8,128)S(1)} %get-tuple-element.14.old_ref, f32[256,128]{1,0:T(8,128)S(1)} %get-tuple-element.15.acc_ref, bf16[256,256]{1,0:T(8,128)(2,1)S(1)} %get-tuple-element.16.same_ref), custom_call_target="tpu_custom_call" | custom-call | flops 33554432 | bytes 524288 | tf_op jit(solution)/shard_map/pick/pallas_call | solution.py:244
  21.6 6.3 %all-to-all-start.1 = ((bf16[16,32,256]{2,1,0:T(8,128)(2,1)}), bf16[16,32,256]{2,1,0:T(8,128)(2,1)S(1)}, u32[]{:S(2)}, u32[]{:S(2)}) async-start(bf16[16,32,256]{2,1,0:T(8,128)(2,1)} %get-tuple-element.17), calls=%async_computation.1 | async-start | bytes 524288 | tf_op jit(solution)/shard_map/all_to_all | solution.py:396
  28.0 2.8 %update.1 = (f32[2048,256]{1,0:T(8,128)}, f32[4,4,128]{2,1,0:T(4,128)}) custom-call(s32[1,256]{1,0:T(1,128)S(1)} %reshape.29.rows_ref, bf16[256,256]{1,0:T(8,128)(2,1)S(1)} %get-tuple-element.18.sums_ref, f32[2048,256]{1,0:T(8,128)S(1)} %copy-done, f32[4,4,128]{2,1,0:T(4,128)S(1)} %bitcast.9), custom_call_target="tpu_custom_call" | custom-call | flops 268435456 | bytes 4194304 | tf_op jit(solution)/shard_map/update/pallas_call | solution.py:294
  30.7 2.2 %all-to-all-done.1 = bf16[16,32,256]{2,1,0:T(8,128)(2,1)S(1)} async-done(((bf16[16,32,256]{2,1,0:T(8,128)(2,1)}), bf16[16,32,256]{2,1,0:T(8,128)(2,1)S(1)}, u32[]{:S(2)}, u32[]{:S(2)}) %all-to-all-start.1) | async-done | bytes 262176 | tf_op jit(solution)/shard_map/all_to_all | solution.py:396
  32.9 0.0 collective-permute-start.1
  32.9 0.7 %first_expand.1.before_ref = bf16[2048,256]{1,0:T(8,128)(2,1)S(1)} custom-call(s16[2048,128]{1,0:T(8,128)(2,1)S(1)} %get-tuple-element.23.cols_ref, bf16[512,256]{1,0:T(8,128)(2,1)S(1)} %bitcast.7), custom_call_target="tpu_custom_call" | custom-call | flops 536870912 | bytes 1310720 | tf_op jit(solution)/shard_map/first_expand/pallas_call | solution.py:356
  33.6 0.8 %collective-permute-done.1.cache_ref = bf16[512,256]{1,0:T(8,128)(2,1)S(1)} collective-permute-done((bf16[512,256]{1,0:T(8,128)(2,1)S(1)}, bf16[512,256]{1,0:T(8,128)(2,1)S(1)}, u32[]{:S(2)}, u32[]{:S(2)}) %collective-permute-start.1) | collective-permute-done | bytes 262176 | tf_op jit(solution)/shard_map/ppermute | solution.py:385
  34.5 1.5 %second_expand.1 = bf16[2048,256]{1,0:T(8,128)(2,1)} custom-call(s16[2048,128]{1,0:T(8,128)(2,1)S(1)} %get-tuple-element.23.cols_ref, bf16[512,256]{1,0:T(8,128)(2,1)S(1)} %collective-permute-done.1.cache_ref, bf16[2048,256]{1,0:T(8,128)(2,1)S(1)} %first_expand.1.before_ref), custom_call_target="tpu_custom_call" | custom-call | flops 536870912 | bytes 1310720 | tf_op jit(solution)/shard_map/second_expand/pallas_call | solution.py:356
  (2 shorter events, 0.0 us)
Async XLA Ops:
  0.6 1.2 %copy-start.2 = (s32[2048]{0:T(1024)S(1)}, s32[2048]{0:T(1024)}, u32[]{:S(2)}) copy-start(s32[2048]{0:T(1024)} %param.8) | copy-start | bytes 24580
  2.6 11.2 %copy-start.3 = (s32[1,8,32]{2,1,0:T(8,128)S(1)}, s32[1,8,32]{2,1,0:T(8,128)}, u32[]{:S(2)}) copy-start(s32[1,8,32]{2,1,0:T(8,128)} %param.9) | copy-start | bytes 3076
  2.6 11.3 %copy-start = (f32[2048,256]{1,0:T(8,128)S(1)}, f32[2048,256]{1,0:T(8,128)}, u32[]{:S(2)}) copy-start(f32[2048,256]{1,0:T(8,128)} %emb_ref.3) | copy-start | bytes 6291460
  2.6 11.3 %copy-start.1 = (f32[2048]{0:T(1024)S(1)}, f32[2048]{0:T(1024)}, u32[]{:S(2)}) copy-start(f32[2048]{0:T(1024)} %param.6) | copy-start | bytes 24580
  2.6 1.7 %collective-permute-start = (bf16[512,256]{1,0:T(8,128)(2,1)S(1)}, bf16[512,256]{1,0:T(8,128)(2,1)S(1)}, u32[]{:S(2)}, u32[]{:S(2)}) collective-permute-start(bf16[512,256]{1,0:T(8,128)(2,1)S(1)} %slot_sums.3), channel_id=1, source_target_pairs={{0,1},{1,0},{2,3},{3,2},{4,5},{5,4},{6,7},{7,6},{8,9},{9,8},{10,11... | collective-permute-start | bytes 786440 | tf_op jit(solution)/shard_map/ppermute | solution.py:385
  5.1 15.5 %all-to-all-start = ((bf16[16,32,256]{2,1,0:T(8,128)(2,1)}), bf16[16,32,256]{2,1,0:T(8,128)(2,1)S(1)}, u32[]{:S(2)}, u32[]{:S(2)}) async-start(bf16[16,32,256]{2,1,0:T(8,128)(2,1)} %bitcast.1), calls=%async_computation | async-start | bytes 524288 | tf_op jit(solution)/shard_map/all_to_all | solution.py:396
  21.6 11.3 %all-to-all-start.1 = ((bf16[16,32,256]{2,1,0:T(8,128)(2,1)}), bf16[16,32,256]{2,1,0:T(8,128)(2,1)S(1)}, u32[]{:S(2)}, u32[]{:S(2)}) async-start(bf16[16,32,256]{2,1,0:T(8,128)(2,1)} %get-tuple-element.17), calls=%async_computation.1 | async-start | bytes 524288 | tf_op jit(solution)/shard_map/all_to_all | solution.py:396
  32.9 1.5 %collective-permute-start.1 = (bf16[512,256]{1,0:T(8,128)(2,1)S(1)}, bf16[512,256]{1,0:T(8,128)(2,1)S(1)}, u32[]{:S(2)}, u32[]{:S(2)}) collective-permute-start(bf16[512,256]{1,0:T(8,128)(2,1)S(1)} %bitcast.6), channel_id=1, source_target_pairs={{0,1},{1,0},{2,3},{3,2},{4,5},{5,4},{6,7},{7,6},{8,9},{9,8},{10,11... | collective-permute-start | bytes 786440 | tf_op jit(solution)/shard_map/ppermute | solution.py:385

commit v3 on v2

--- a/solution.py
+++ b/solution.py
@@ -26,7 +26,9 @@
     mid = n_z // 2
     if back:
         zs = [*range(mid, n_z), *reversed(range(mid))]
-        return [z * n_yx + yx for z in zs for yx in reversed(range(n_yx))]
+        path = [z * n_yx + yx for z in zs for yx in reversed(range(n_yx))]
+        first = n_yx // 2
+        return path[first:] + path[:first]
     zs = [*reversed(range(mid + 1)), *reversed(range(mid + 1, n_z))]
     return [z * n_yx + (at ^ (n_yx // 2)) for at in range(n_yx) for z in zs]
 

time: 36.4 us -> 36.9 us (1.014)
  waiting for transfers between devices: 9.1 us -> 10.4 us
  starting transfers between devices: 15.6 us -> 14.8 us
    all_to_all x2, waiting for transfers between devices: 7.83 us -> 9.12 us  [exchange(): lax.all_to_all(blocks, ('hst', 'x'), split_axis=0, concat_axis=0, axis_in...]
    all_to_all x2, starting transfers between devices: 15.1 us -> 14.3 us  [exchange(): lax.all_to_all(blocks, ('hst', 'x'), split_axis=0, concat_axis=0, axis_in...]
  transfers between devices with their start and end apart: 4 -> 4, of which waited for: 4 -> 4; matrix products, arithmetic and copies ran while one was open for 0% -> 0% of each run, Pallas kernels for 15% -> 14%
where the time goes in v3:
time: 36.9 us; the launch traced here: 36.5 us
  starting transfers between devices  14.8 us (40%)
  Pallas kernels  10.5 us (28%)
  waiting for transfers between devices  10.4 us (28%)
  between operations  0.73 us (2%)
    all_to_all x2, starting transfers between devices, exchange(): lax.all_to_all(blocks, ('hst', 'x'), split_axis=0, concat_axis=0, axis_in...  14.3 us
    all_to_all x2, waiting for transfers between devices, exchange(): lax.all_to_all(blocks, ('hst', 'x'), split_axis=0, concat_axis=0, axis_in...  9.12 us
    pallas_call x1, Pallas kernels, update(): pl.pallas_call(update_kernel, grid=(steps,), in_specs=[pl.BlockSpec((1, s...  2.76 us
    pallas_call x2, Pallas kernels, expand(): pl.pallas_call(second_expand_kernel if last else first_expand_kernel, in_...  2.23 us
    pallas_call x2, Pallas kernels, slot_sums(): pl.pallas_call(functools.partial(sums_kernel, base=base, half=half, capac...  1.41 us
    ppermute x2, waiting for transfers between devices, swap(): return lax.ppermute(block, 'core', [(0, 1), (1, 0)])  1.27 us
    pallas_call x1, Pallas kernels, load(): pl.pallas_call(load_kernel, in_specs=[pl.BlockSpec(memory_space=pl.ANY)],...  1.22 us
    pallas_call x1, Pallas kernels, prepare(): pl.pallas_call(functools.partial(prepare_kernel, half=half, capacity=capa...  1.08 us
  transfers between devices with their start and end apart: 4, of which 4 were waited for; matrix products, arithmetic and copies ran while one was open for 0% of the time, Pallas kernels for 14%

profile of v3, /device:TPU:0, one launch (start us, length us, event | category | flops | bytes accessed | tf_op | source)
XLA Modules:
  0.0 36.5 jit_solution(17254007303033288467)
XLA Ops:
  0.6 0.0 copy-start.2
  0.6 1.2 %load.1.grads_ref = bf16[2048,256]{1,0:T(8,128)(2,1)S(1)} custom-call(bf16[2048,256]{1,0:T(8,128)(2,1)} %grads_ref.1), custom_call_target="tpu_custom_call" | custom-call | bytes 2097152 | tf_op jit(solution)/shard_map/load/pallas_call | solution.py:80
  1.9 0.0 copy-done.2
  1.9 0.7 %slot_sums.3 = bf16[512,256]{1,0:T(8,128)(2,1)S(1)} custom-call(s32[1,2048]{1,0:T(1,128)S(1)} %bitcast.10, bf16[2048,256]{1,0:T(8,128)(2,1)S(1)} %load.1.grads_ref), custom_call_target="tpu_custom_call" | custom-call | flops 536870912 | bytes 1310720 | tf_op jit(solution)/shard_map/slot_sums/pallas_call | solution.py:105
  2.6 0.0 copy-start.3
  2.6 0.0 copy-start
  2.6 0.0 copy-start.1
  2.6 0.5 %collective-permute-start = (bf16[512,256]{1,0:T(8,128)(2,1)S(1)}, bf16[512,256]{1,0:T(8,128)(2,1)S(1)}, u32[]{:S(2)}, u32[]{:S(2)}) collective-permute-start(bf16[512,256]{1,0:T(8,128)(2,1)S(1)} %slot_sums.3), channel_id=1, source_target_pairs={{0,1},{1,0},{2,3},{3,2},{4,5},{5,4},{6,7},{7,6},{8,9},{9,8},{10,11... | collective-permute-start | bytes 786440 | tf_op jit(solution)/shard_map/ppermute | solution.py:387
  3.1 0.7 %slot_sums.2.a_ref = bf16[512,256]{1,0:T(8,128)(2,1)S(1)} custom-call(s32[1,2048]{1,0:T(1,128)S(1)} %bitcast.11, bf16[2048,256]{1,0:T(8,128)(2,1)S(1)} %load.1.grads_ref), custom_call_target="tpu_custom_call" | custom-call | flops 536870912 | bytes 1310720 | tf_op jit(solution)/shard_map/slot_sums/pallas_call | solution.py:105
  3.9 0.5 %collective-permute-done.b_ref = bf16[512,256]{1,0:T(8,128)(2,1)S(1)} collective-permute-done((bf16[512,256]{1,0:T(8,128)(2,1)S(1)}, bf16[512,256]{1,0:T(8,128)(2,1)S(1)}, u32[]{:S(2)}, u32[]{:S(2)}) %collective-permute-start) | collective-permute-done | bytes 262176 | tf_op jit(solution)/shard_map/ppermute | solution.py:387
  4.3 0.7 %add.1 = bf16[512,256]{1,0:T(8,128)(2,1)} custom-call(bf16[512,256]{1,0:T(8,128)(2,1)S(1)} %slot_sums.2.a_ref, bf16[512,256]{1,0:T(8,128)(2,1)S(1)} %collective-permute-done.b_ref), custom_call_target="tpu_custom_call" | custom-call | flops 131072 | bytes 786432 | tf_op jit(solution)/shard_map/add/pallas_call | solution.py:143
  5.1 8.7 %all-to-all-start = ((bf16[16,32,256]{2,1,0:T(8,128)(2,1)}), bf16[16,32,256]{2,1,0:T(8,128)(2,1)S(1)}, u32[]{:S(2)}, u32[]{:S(2)}) async-start(bf16[16,32,256]{2,1,0:T(8,128)(2,1)} %bitcast.1), calls=%async_computation | async-start | bytes 524288 | tf_op jit(solution)/shard_map/all_to_all | solution.py:398
  13.8 0.1 reshape.29.rows_ref
  13.9 0.0 copy-done.1
  13.9 1.1 %prepare.1 = (f32[256,256]{1,0:T(8,128)S(1)}, f32[256,128]{1,0:T(8,128)S(1)}, bf16[256,256]{1,0:T(8,128)(2,1)S(1)}, s16[2048,128]{1,0:T(8,128)(2,1)S(1)}) custom-call(s32[1,256]{1,0:T(1,128)S(1)} %reshape.29.rows_ref, f32[2048,256]{1,0:T(8,128)S(1)} %copy-done, f32[16,128]{1,0:T(8,128)S(1)} %bitcast.8, s32[1,2048]{1,0:T(1,128)S(1)} %bitcast.12), custom_call_target="tpu_custom_call" | custom-call | flops 536870912 | bytes 2097152 | tf_op jit(solution)/shard_map/prepare/pallas_call | solution.py:196
  15.0 5.6 %all-to-all-done.arrived_ref = bf16[16,32,256]{2,1,0:T(8,128)(2,1)S(1)} async-done(((bf16[16,32,256]{2,1,0:T(8,128)(2,1)}), bf16[16,32,256]{2,1,0:T(8,128)(2,1)S(1)}, u32[]{:S(2)}, u32[]{:S(2)}) %all-to-all-start) | async-done | bytes 262176 | tf_op jit(solution)/shard_map/all_to_all | solution.py:398
  20.6 1.0 %pick.1 = (bf16[16,32,256]{2,1,0:T(8,128)(2,1)}, bf16[256,256]{1,0:T(8,128)(2,1)S(1)}) custom-call(bf16[16,32,256]{2,1,0:T(8,128)(2,1)S(1)} %all-to-all-done.arrived_ref, f32[256,256]{1,0:T(8,128)S(1)} %get-tuple-element.14.old_ref, f32[256,128]{1,0:T(8,128)S(1)} %get-tuple-element.15.acc_ref, bf16[256,256]{1,0:T(8,128)(2,1)S(1)} %get-tuple-element.16.same_ref), custom_call_target="tpu_custom_call" | custom-call | flops 33554432 | bytes 524288 | tf_op jit(solution)/shard_map/pick/pallas_call | solution.py:246
  21.6 5.6 %all-to-all-start.1 = ((bf16[16,32,256]{2,1,0:T(8,128)(2,1)}), bf16[16,32,256]{2,1,0:T(8,128)(2,1)S(1)}, u32[]{:S(2)}, u32[]{:S(2)}) async-start(bf16[16,32,256]{2,1,0:T(8,128)(2,1)} %get-tuple-element.17), calls=%async_computation.1 | async-start | bytes 524288 | tf_op jit(solution)/shard_map/all_to_all | solution.py:398
  27.2 2.8 %update.1 = (f32[2048,256]{1,0:T(8,128)}, f32[4,4,128]{2,1,0:T(4,128)}) custom-call(s32[1,256]{1,0:T(1,128)S(1)} %reshape.29.rows_ref, bf16[256,256]{1,0:T(8,128)(2,1)S(1)} %get-tuple-element.18.sums_ref, f32[2048,256]{1,0:T(8,128)S(1)} %copy-done, f32[4,4,128]{2,1,0:T(4,128)S(1)} %bitcast.9), custom_call_target="tpu_custom_call" | custom-call | flops 268435456 | bytes 4194304 | tf_op jit(solution)/shard_map/update/pallas_call | solution.py:296
  30.0 3.5 %all-to-all-done.1 = bf16[16,32,256]{2,1,0:T(8,128)(2,1)S(1)} async-done(((bf16[16,32,256]{2,1,0:T(8,128)(2,1)}), bf16[16,32,256]{2,1,0:T(8,128)(2,1)S(1)}, u32[]{:S(2)}, u32[]{:S(2)}) %all-to-all-start.1) | async-done | bytes 262176 | tf_op jit(solution)/shard_map/all_to_all | solution.py:398
  33.5 0.0 collective-permute-start.1
  33.5 0.7 %first_expand.1.before_ref = bf16[2048,256]{1,0:T(8,128)(2,1)S(1)} custom-call(s16[2048,128]{1,0:T(8,128)(2,1)S(1)} %get-tuple-element.23.cols_ref, bf16[512,256]{1,0:T(8,128)(2,1)S(1)} %bitcast.7), custom_call_target="tpu_custom_call" | custom-call | flops 536870912 | bytes 1310720 | tf_op jit(solution)/shard_map/first_expand/pallas_call | solution.py:358
  34.2 0.8 %collective-permute-done.1.cache_ref = bf16[512,256]{1,0:T(8,128)(2,1)S(1)} collective-permute-done((bf16[512,256]{1,0:T(8,128)(2,1)S(1)}, bf16[512,256]{1,0:T(8,128)(2,1)S(1)}, u32[]{:S(2)}, u32[]{:S(2)}) %collective-permute-start.1) | collective-permute-done | bytes 262176 | tf_op jit(solution)/shard_map/ppermute | solution.py:387
  35.0 1.5 %second_expand.1 = bf16[2048,256]{1,0:T(8,128)(2,1)} custom-call(s16[2048,128]{1,0:T(8,128)(2,1)S(1)} %get-tuple-element.23.cols_ref, bf16[512,256]{1,0:T(8,128)(2,1)S(1)} %collective-permute-done.1.cache_ref, bf16[2048,256]{1,0:T(8,128)(2,1)S(1)} %first_expand.1.before_ref), custom_call_target="tpu_custom_call" | custom-call | flops 536870912 | bytes 1310720 | tf_op jit(solution)/shard_map/second_expand/pallas_call | solution.py:358
  (2 shorter events, 0.0 us)
Async XLA Ops:
  0.6 1.2 %copy-start.2 = (s32[2048]{0:T(1024)S(1)}, s32[2048]{0:T(1024)}, u32[]{:S(2)}) copy-start(s32[2048]{0:T(1024)} %param.8) | copy-start | bytes 24580
  2.6 11.2 %copy-start.3 = (s32[1,8,32]{2,1,0:T(8,128)S(1)}, s32[1,8,32]{2,1,0:T(8,128)}, u32[]{:S(2)}) copy-start(s32[1,8,32]{2,1,0:T(8,128)} %param.9) | copy-start | bytes 3076
  2.6 11.3 %copy-start = (f32[2048,256]{1,0:T(8,128)S(1)}, f32[2048,256]{1,0:T(8,128)}, u32[]{:S(2)}) copy-start(f32[2048,256]{1,0:T(8,128)} %emb_ref.3) | copy-start | bytes 6291460
  2.6 11.3 %copy-start.1 = (f32[2048]{0:T(1024)S(1)}, f32[2048]{0:T(1024)}, u32[]{:S(2)}) copy-start(f32[2048]{0:T(1024)} %param.6) | copy-start | bytes 24580
  2.6 1.7 %collective-permute-start = (bf16[512,256]{1,0:T(8,128)(2,1)S(1)}, bf16[512,256]{1,0:T(8,128)(2,1)S(1)}, u32[]{:S(2)}, u32[]{:S(2)}) collective-permute-start(bf16[512,256]{1,0:T(8,128)(2,1)S(1)} %slot_sums.3), channel_id=1, source_target_pairs={{0,1},{1,0},{2,3},{3,2},{4,5},{5,4},{6,7},{7,6},{8,9},{9,8},{10,11... | collective-permute-start | bytes 786440 | tf_op jit(solution)/shard_map/ppermute | solution.py:387
  5.1 15.5 %all-to-all-start = ((bf16[16,32,256]{2,1,0:T(8,128)(2,1)}), bf16[16,32,256]{2,1,0:T(8,128)(2,1)S(1)}, u32[]{:S(2)}, u32[]{:S(2)}) async-start(bf16[16,32,256]{2,1,0:T(8,128)(2,1)} %bitcast.1), calls=%async_computation | async-start | bytes 524288 | tf_op jit(solution)/shard_map/all_to_all | solution.py:398
  21.6 11.8 %all-to-all-start.1 = ((bf16[16,32,256]{2,1,0:T(8,128)(2,1)}), bf16[16,32,256]{2,1,0:T(8,128)(2,1)S(1)}, u32[]{:S(2)}, u32[]{:S(2)}) async-start(bf16[16,32,256]{2,1,0:T(8,128)(2,1)} %get-tuple-element.17), calls=%async_computation.1 | async-start | bytes 524288 | tf_op jit(solution)/shard_map/all_to_all | solution.py:398
  33.5 1.5 %collective-permute-start.1 = (bf16[512,256]{1,0:T(8,128)(2,1)S(1)}, bf16[512,256]{1,0:T(8,128)(2,1)S(1)}, u32[]{:S(2)}, u32[]{:S(2)}) collective-permute-start(bf16[512,256]{1,0:T(8,128)(2,1)S(1)} %bitcast.6), channel_id=1, source_target_pairs={{0,1},{1,0},{2,3},{3,2},{4,5},{5,4},{6,7},{7,6},{8,9},{9,8},{10,11... | collective-permute-start | bytes 786440 | tf_op jit(solution)/shard_map/ppermute | solution.py:387

commit v4 on v1

--- a/solution.py
+++ b/solution.py
@@ -20,26 +20,27 @@
     return 1 << (bits_of(n_hst) // 2)
 
 
-def z_place(z, n_z, back):
-    return (z - n_z // 2 if back else n_z // 2 - z) & (n_z - 1)
+def chip_place(z, yx, n_z, n_yx, back):
+    if back:
+        return ((z + n_z // 2) & (n_z - 1)) * n_yx + (n_yx - 1 - yx)
+    return (yx ^ (n_yx // 2)) * n_z + ((n_z // 2 - z) & (n_z - 1))
 
 
 def member(host, chip, n_hst, chips, back):
     n_y = planes(n_hst)
-    n_z = n_hst // n_y
-    z, y = host // n_y, host % n_y
-    return (y * chips + chip) * n_z + z_place(z, n_z, back)
+    return chip_place(host // n_y, host % n_y * chips + chip, n_hst // n_y, n_y * chips, back)
 
 
 def slot_place(ids, capacity, half, back):
     n_hst, chips = lax.axis_size("hst"), lax.axis_size("x")
-    n_y = planes(n_hst)
-    n_z = n_hst // n_y
-    cap_bits, z_bits, yx_bits = bits_of(capacity), bits_of(n_z), bits_of(n_y * chips)
+    n_yx = planes(n_hst) * chips
+    cap_bits = bits_of(capacity)
     other = ((ids >> cap_bits) & 1) ^ lax.axis_index("core")
-    z = z_place(ids >> (cap_bits + 1 + yx_bits), n_z, back)
-    yx = (ids >> (cap_bits + 1)) & ((1 << yx_bits) - 1)
-    return other * half + (((yx << z_bits) + z) << cap_bits) + (ids & (capacity - 1))
+    chip = ids >> (cap_bits + 1)
+    place = chip_place(
+        chip >> bits_of(n_yx), chip & (n_yx - 1), n_hst * chips // n_yx, n_yx, back
+    )
+    return other * half + (place << cap_bits) + (ids & (capacity - 1))
 
 
 def column(row):
@@ -56,11 +57,13 @@
 
 def onehot_lines(place, block):
     shape = (16, place.shape[1])
-    slot = small(lax.broadcasted_iota(jnp.int32, shape, 0))
+    slot = lax.broadcasted_iota(jnp.int32, (16, 128), 0)
     place = small(jnp.broadcast_to(place, shape))
-    return jnp.concatenate(
-        [matches(slot, place - jnp.int16(start)) for start in range(0, block, 16)], axis=0
-    )
+    lines = []
+    for start in range(0, block, 16):
+        here = small(slot + start)
+        lines.append(matches(jnp.concatenate([here] * (shape[1] // 128), axis=1), place))
+    return jnp.concatenate(lines, axis=0)
 
 
 def load_kernel(grads_ref, out_ref, sems):
@@ -81,7 +84,7 @@
         in_specs=[pl.BlockSpec(memory_space=pl.ANY)],
         out_specs=pl.BlockSpec(memory_space=pltpu.VMEM),
         out_shape=jax.ShapeDtypeStruct(grads.shape, grads.dtype),
-        scratch_shapes=[pltpu.SemaphoreType.DMA((16,))],
+        scratch_shapes=[pltpu.SemaphoreType.DMA((2,))],
         compiler_params=pltpu.CompilerParams(vmem_limit_bytes=52 * MIB),
         cost_estimate=pl.CostEstimate(
             flops=0, bytes_accessed=4 * grads.shape[0] * grads.shape[1], transcendentals=0
@@ -318,19 +321,22 @@
 
 
 def chosen_rows(cols, cache, base):
-    slots = cache.shape[0]
-    lane = lax.broadcasted_iota(jnp.int32, cols.shape, 1)
-    onehot = jnp.concatenate(
-        [matches(cols, small(lane + (base + start))) for start in range(0, slots, 128)], axis=1
-    )
-    return jnp.dot(onehot, cache, preferred_element_type=jnp.float32)
+    lookups = cols.shape[0]
+    lane = lax.broadcasted_iota(jnp.int32, (16, 128), 1)
+    tiles = []
+    for start in range(0, cache.shape[0], 128):
+        here = small(lane + (base + start))
+        tiles.append(matches(cols, jnp.concatenate([here] * (lookups // 16), axis=0)))
+    return jnp.dot(
+        jnp.concatenate(tiles, axis=1), cache, preferred_element_type=jnp.float32
+    ).astype(jnp.bfloat16)
 
 
 def first_expand_kernel(cols_ref, cache_ref, out_ref):
     block = min(1024, MIB // cache_ref.shape[0])
     for start in range(0, out_ref.shape[0], block):
         at = slice(start, start + block)
-        out_ref[at, :] = chosen_rows(cols_ref[at, :], cache_ref[...], 0).astype(jnp.bfloat16)
+        out_ref[at, :] = chosen_rows(cols_ref[at, :], cache_ref[...], 0)
 
 
 def second_expand_kernel(cols_ref, cache_ref, before_ref, out_ref, lines, sems):
@@ -339,7 +345,7 @@
     for start in range(0, lines.shape[0], block):
         at = slice(start, start + block)
         rows = chosen_rows(cols_ref[at, :], cache_ref[...], cache_ref.shape[0])
-        lines[at, :] = (rows + before_ref[at, :].astype(jnp.float32)).astype(jnp.bfloat16)
+        lines[at, :] = rows + before_ref[at, :]
         window = pl.ds(start, block)
         copies.append(
             pltpu.make_async_copy(lines.at[window], out_ref.at[window], sems.at[start // block])

time: 37.5 us -> 35.9 us (0.957)
  waiting for transfers between devices: 10.3 us -> 8.72 us
    all_to_all x2, waiting for transfers between devices: 8.99 us -> 7.45 us  [exchange(): lax.all_to_all(blocks, ('hst', 'x'), split_axis=0, concat_axis=0, axis_in...]
  transfers between devices with their start and end apart: 4 -> 4, of which waited for: 4 -> 4; matrix products, arithmetic and copies ran while one was open for 0% -> 0% of each run, Pallas kernels for 14% -> 15%
where the time goes in v4:
time: 35.9 us; the launch traced here: 35.5 us
  starting transfers between devices  15.5 us (43%)
  Pallas kernels  10.4 us (29%)
  waiting for transfers between devices  8.72 us (24%)
  between operations  0.73 us (2%)
    all_to_all x2, starting transfers between devices, exchange(): lax.all_to_all(blocks, ('hst', 'x'), split_axis=0, concat_axis=0, axis_in...  15 us
    all_to_all x2, waiting for transfers between devices, exchange(): lax.all_to_all(blocks, ('hst', 'x'), split_axis=0, concat_axis=0, axis_in...  7.45 us
    pallas_call x1, Pallas kernels, update(): pl.pallas_call(update_kernel, grid=(steps,), in_specs=[pl.BlockSpec((1, s...  2.75 us
    pallas_call x2, Pallas kernels, expand(): pl.pallas_call(second_expand_kernel if last else first_expand_kernel, in_...  2.19 us
    pallas_call x2, Pallas kernels, slot_sums(): pl.pallas_call(functools.partial(sums_kernel, base=base, half=half, capac...  1.42 us
    ppermute x2, waiting for transfers between devices, swap(): return lax.ppermute(block, 'core', [(0, 1), (1, 0)])  1.27 us
    pallas_call x1, Pallas kernels, load(): pl.pallas_call(load_kernel, in_specs=[pl.BlockSpec(memory_space=pl.ANY)],...  1.22 us
    pallas_call x1, Pallas kernels, prepare(): pl.pallas_call(functools.partial(prepare_kernel, half=half, capacity=capa...  1.07 us
  transfers between devices with their start and end apart: 4, of which 4 were waited for; matrix products, arithmetic and copies ran while one was open for 0% of the time, Pallas kernels for 15%

profile of v4, /device:TPU:0, one launch (start us, length us, event | category | flops | bytes accessed | tf_op | source)
XLA Modules:
  0.0 35.5 jit_solution(16044518479961302774)
XLA Ops:
  0.6 0.0 copy-start.2
  0.6 1.2 %load.1.grads_ref = bf16[2048,256]{1,0:T(8,128)(2,1)S(1)} custom-call(bf16[2048,256]{1,0:T(8,128)(2,1)} %grads_ref.1), custom_call_target="tpu_custom_call" | custom-call | bytes 2097152 | tf_op jit(solution)/shard_map/load/pallas_call | solution.py:82
  1.9 0.0 copy-done.2
  1.9 0.7 %slot_sums.3 = bf16[512,256]{1,0:T(8,128)(2,1)S(1)} custom-call(s32[1,2048]{1,0:T(1,128)S(1)} %bitcast.10, bf16[2048,256]{1,0:T(8,128)(2,1)S(1)} %load.1.grads_ref), custom_call_target="tpu_custom_call" | custom-call | flops 536870912 | bytes 1310720 | tf_op jit(solution)/shard_map/slot_sums/pallas_call | solution.py:107
  2.6 0.0 copy-start.3
  2.6 0.0 copy-start
  2.6 0.0 copy-start.1
  2.6 0.5 %collective-permute-start = (bf16[512,256]{1,0:T(8,128)(2,1)S(1)}, bf16[512,256]{1,0:T(8,128)(2,1)S(1)}, u32[]{:S(2)}, u32[]{:S(2)}) collective-permute-start(bf16[512,256]{1,0:T(8,128)(2,1)S(1)} %slot_sums.3), channel_id=1, source_target_pairs={{0,1},{1,0},{2,3},{3,2},{4,5},{5,4},{6,7},{7,6},{8,9},{9,8},{10,11... | collective-permute-start | bytes 786440 | tf_op jit(solution)/shard_map/ppermute | solution.py:392
  3.1 0.7 %slot_sums.2.a_ref = bf16[512,256]{1,0:T(8,128)(2,1)S(1)} custom-call(s32[1,2048]{1,0:T(1,128)S(1)} %bitcast.11, bf16[2048,256]{1,0:T(8,128)(2,1)S(1)} %load.1.grads_ref), custom_call_target="tpu_custom_call" | custom-call | flops 536870912 | bytes 1310720 | tf_op jit(solution)/shard_map/slot_sums/pallas_call | solution.py:107
  3.9 0.4 %collective-permute-done.b_ref = bf16[512,256]{1,0:T(8,128)(2,1)S(1)} collective-permute-done((bf16[512,256]{1,0:T(8,128)(2,1)S(1)}, bf16[512,256]{1,0:T(8,128)(2,1)S(1)}, u32[]{:S(2)}, u32[]{:S(2)}) %collective-permute-start) | collective-permute-done | bytes 262176 | tf_op jit(solution)/shard_map/ppermute | solution.py:392
  4.3 0.7 %add.1 = bf16[512,256]{1,0:T(8,128)(2,1)} custom-call(bf16[512,256]{1,0:T(8,128)(2,1)S(1)} %slot_sums.2.a_ref, bf16[512,256]{1,0:T(8,128)(2,1)S(1)} %collective-permute-done.b_ref), custom_call_target="tpu_custom_call" | custom-call | flops 131072 | bytes 786432 | tf_op jit(solution)/shard_map/add/pallas_call | solution.py:145
  5.1 8.7 %all-to-all-start = ((bf16[16,32,256]{2,1,0:T(8,128)(2,1)}), bf16[16,32,256]{2,1,0:T(8,128)(2,1)S(1)}, u32[]{:S(2)}, u32[]{:S(2)}) async-start(bf16[16,32,256]{2,1,0:T(8,128)(2,1)} %bitcast.1), calls=%async_computation | async-start | bytes 524288 | tf_op jit(solution)/shard_map/all_to_all | solution.py:405
  13.8 0.1 reshape.29.rows_ref
  13.9 0.0 copy-done.1
  13.9 1.1 %prepare.1 = (f32[256,256]{1,0:T(8,128)S(1)}, f32[256,128]{1,0:T(8,128)S(1)}, bf16[256,256]{1,0:T(8,128)(2,1)S(1)}, s16[2048,128]{1,0:T(8,128)(2,1)S(1)}) custom-call(s32[1,256]{1,0:T(1,128)S(1)} %reshape.29.rows_ref, f32[2048,256]{1,0:T(8,128)S(1)} %copy-done, f32[16,128]{1,0:T(8,128)S(1)} %bitcast.8, s32[1,2048]{1,0:T(1,128)S(1)} %bitcast.12), custom_call_target="tpu_custom_call" | custom-call | flops 536870912 | bytes 2097152 | tf_op jit(solution)/shard_map/prepare/pallas_call | solution.py:198
  15.0 5.6 %all-to-all-done.arrived_ref = bf16[16,32,256]{2,1,0:T(8,128)(2,1)S(1)} async-done(((bf16[16,32,256]{2,1,0:T(8,128)(2,1)}), bf16[16,32,256]{2,1,0:T(8,128)(2,1)S(1)}, u32[]{:S(2)}, u32[]{:S(2)}) %all-to-all-start) | async-done | bytes 262176 | tf_op jit(solution)/shard_map/all_to_all | solution.py:405
  20.6 1.0 %pick.1 = (bf16[16,32,256]{2,1,0:T(8,128)(2,1)}, bf16[256,256]{1,0:T(8,128)(2,1)S(1)}) custom-call(bf16[16,32,256]{2,1,0:T(8,128)(2,1)S(1)} %all-to-all-done.arrived_ref, f32[256,256]{1,0:T(8,128)S(1)} %get-tuple-element.14.old_ref, f32[256,128]{1,0:T(8,128)S(1)} %get-tuple-element.15.acc_ref, bf16[256,256]{1,0:T(8,128)(2,1)S(1)} %get-tuple-element.16.same_ref), custom_call_target="tpu_custom_call" | custom-call | flops 33554432 | bytes 524288 | tf_op jit(solution)/shard_map/pick/pallas_call | solution.py:248
  21.6 6.3 %all-to-all-start.1 = ((bf16[16,32,256]{2,1,0:T(8,128)(2,1)}), bf16[16,32,256]{2,1,0:T(8,128)(2,1)S(1)}, u32[]{:S(2)}, u32[]{:S(2)}) async-start(bf16[16,32,256]{2,1,0:T(8,128)(2,1)} %get-tuple-element.17), calls=%async_computation.1 | async-start | bytes 524288 | tf_op jit(solution)/shard_map/all_to_all | solution.py:405
  27.9 2.7 %update.1 = (f32[2048,256]{1,0:T(8,128)}, f32[4,4,128]{2,1,0:T(4,128)}) custom-call(s32[1,256]{1,0:T(1,128)S(1)} %reshape.29.rows_ref, bf16[256,256]{1,0:T(8,128)(2,1)S(1)} %get-tuple-element.18.sums_ref, f32[2048,256]{1,0:T(8,128)S(1)} %copy-done, f32[4,4,128]{2,1,0:T(4,128)S(1)} %bitcast.9), custom_call_target="tpu_custom_call" | custom-call | flops 268435456 | bytes 4194304 | tf_op jit(solution)/shard_map/update/pallas_call | solution.py:298
  30.7 1.8 %all-to-all-done.1 = bf16[16,32,256]{2,1,0:T(8,128)(2,1)S(1)} async-done(((bf16[16,32,256]{2,1,0:T(8,128)(2,1)}), bf16[16,32,256]{2,1,0:T(8,128)(2,1)S(1)}, u32[]{:S(2)}, u32[]{:S(2)}) %all-to-all-start.1) | async-done | bytes 262176 | tf_op jit(solution)/shard_map/all_to_all | solution.py:405
  32.5 0.0 collective-permute-start.1
  32.5 0.7 %first_expand.1.before_ref = bf16[2048,256]{1,0:T(8,128)(2,1)S(1)} custom-call(s16[2048,128]{1,0:T(8,128)(2,1)S(1)} %get-tuple-element.23.cols_ref, bf16[512,256]{1,0:T(8,128)(2,1)S(1)} %bitcast.7), custom_call_target="tpu_custom_call" | custom-call | flops 536870912 | bytes 1310720 | tf_op jit(solution)/shard_map/first_expand/pallas_call | solution.py:363
  33.2 0.8 %collective-permute-done.1.cache_ref = bf16[512,256]{1,0:T(8,128)(2,1)S(1)} collective-permute-done((bf16[512,256]{1,0:T(8,128)(2,1)S(1)}, bf16[512,256]{1,0:T(8,128)(2,1)S(1)}, u32[]{:S(2)}, u32[]{:S(2)}) %collective-permute-start.1) | collective-permute-done | bytes 262176 | tf_op jit(solution)/shard_map/ppermute | solution.py:392
  34.0 1.5 %second_expand.1 = bf16[2048,256]{1,0:T(8,128)(2,1)} custom-call(s16[2048,128]{1,0:T(8,128)(2,1)S(1)} %get-tuple-element.23.cols_ref, bf16[512,256]{1,0:T(8,128)(2,1)S(1)} %collective-permute-done.1.cache_ref, bf16[2048,256]{1,0:T(8,128)(2,1)S(1)} %first_expand.1.before_ref), custom_call_target="tpu_custom_call" | custom-call | flops 536870912 | bytes 1310720 | tf_op jit(solution)/shard_map/second_expand/pallas_call | solution.py:363
  (2 shorter events, 0.0 us)
Async XLA Ops:
  0.6 1.2 %copy-start.2 = (s32[2048]{0:T(1024)S(1)}, s32[2048]{0:T(1024)}, u32[]{:S(2)}) copy-start(s32[2048]{0:T(1024)} %param.8) | copy-start | bytes 24580
  2.6 11.2 %copy-start.3 = (s32[1,8,32]{2,1,0:T(8,128)S(1)}, s32[1,8,32]{2,1,0:T(8,128)}, u32[]{:S(2)}) copy-start(s32[1,8,32]{2,1,0:T(8,128)} %param.9) | copy-start | bytes 3076
  2.6 11.3 %copy-start = (f32[2048,256]{1,0:T(8,128)S(1)}, f32[2048,256]{1,0:T(8,128)}, u32[]{:S(2)}) copy-start(f32[2048,256]{1,0:T(8,128)} %emb_ref.3) | copy-start | bytes 6291460
  2.6 11.3 %copy-start.1 = (f32[2048]{0:T(1024)S(1)}, f32[2048]{0:T(1024)}, u32[]{:S(2)}) copy-start(f32[2048]{0:T(1024)} %param.6) | copy-start | bytes 24580
  2.6 1.7 %collective-permute-start = (bf16[512,256]{1,0:T(8,128)(2,1)S(1)}, bf16[512,256]{1,0:T(8,128)(2,1)S(1)}, u32[]{:S(2)}, u32[]{:S(2)}) collective-permute-start(bf16[512,256]{1,0:T(8,128)(2,1)S(1)} %slot_sums.3), channel_id=1, source_target_pairs={{0,1},{1,0},{2,3},{3,2},{4,5},{5,4},{6,7},{7,6},{8,9},{9,8},{10,11... | collective-permute-start | bytes 786440 | tf_op jit(solution)/shard_map/ppermute | solution.py:392
  5.1 15.5 %all-to-all-start = ((bf16[16,32,256]{2,1,0:T(8,128)(2,1)}), bf16[16,32,256]{2,1,0:T(8,128)(2,1)S(1)}, u32[]{:S(2)}, u32[]{:S(2)}) async-start(bf16[16,32,256]{2,1,0:T(8,128)(2,1)} %bitcast.1), calls=%async_computation | async-start | bytes 524288 | tf_op jit(solution)/shard_map/all_to_all | solution.py:405
  21.6 10.9 %all-to-all-start.1 = ((bf16[16,32,256]{2,1,0:T(8,128)(2,1)}), bf16[16,32,256]{2,1,0:T(8,128)(2,1)S(1)}, u32[]{:S(2)}, u32[]{:S(2)}) async-start(bf16[16,32,256]{2,1,0:T(8,128)(2,1)} %get-tuple-element.17), calls=%async_computation.1 | async-start | bytes 524288 | tf_op jit(solution)/shard_map/all_to_all | solution.py:405
  32.5 1.5 %collective-permute-start.1 = (bf16[512,256]{1,0:T(8,128)(2,1)S(1)}, bf16[512,256]{1,0:T(8,128)(2,1)S(1)}, u32[]{:S(2)}, u32[]{:S(2)}) collective-permute-start(bf16[512,256]{1,0:T(8,128)(2,1)S(1)} %bitcast.6), channel_id=1, source_target_pairs={{0,1},{1,0},{2,3},{3,2},{4,5},{5,4},{6,7},{7,6},{8,9},{9,8},{10,11... | collective-permute-start | bytes 786440 | tf_op jit(solution)/shard_map/ppermute | solution.py:392

commit v5 on v4

--- a/solution.py
+++ b/solution.py
@@ -20,26 +20,26 @@
     return 1 << (bits_of(n_hst) // 2)
 
 
-def chip_place(z, yx, n_z, n_yx, back):
+def chip_order(n_hst, chips, back):
+    n_y = planes(n_hst)
+    n_z, n_yx = n_hst // n_y, n_y * chips
+    mid = n_z // 2
     if back:
-        return ((z + n_z // 2) & (n_z - 1)) * n_yx + (n_yx - 1 - yx)
-    return (yx ^ (n_yx // 2)) * n_z + ((n_z // 2 - z) & (n_z - 1))
-
-
-def member(host, chip, n_hst, chips, back):
-    n_y = planes(n_hst)
-    return chip_place(host // n_y, host % n_y * chips + chip, n_hst // n_y, n_y * chips, back)
+        zs = [(mid + step) % n_z for step in range(n_z)]
+        yxs = [*reversed(range(1, n_yx, 2)), *reversed(range(0, n_yx, 2))]
+        return [z * n_yx + yx for z in zs for yx in yxs]
+    zs = [(mid - step) % n_z for step in range(n_z)]
+    yxs = [*range(n_yx // 2, n_yx), *reversed(range(n_yx // 2))]
+    return [z * n_yx + yx for yx in yxs for z in zs]
 
 
 def slot_place(ids, capacity, half, back):
-    n_hst, chips = lax.axis_size("hst"), lax.axis_size("x")
-    n_yx = planes(n_hst) * chips
     cap_bits = bits_of(capacity)
     other = ((ids >> cap_bits) & 1) ^ lax.axis_index("core")
     chip = ids >> (cap_bits + 1)
-    place = chip_place(
-        chip >> bits_of(n_yx), chip & (n_yx - 1), n_hst * chips // n_yx, n_yx, back
-    )
+    place = jnp.zeros_like(chip)
+    for at, member in enumerate(chip_order(lax.axis_size("hst"), lax.axis_size("x"), back)):
+        place = jnp.where(chip == member, at, place)
     return other * half + (place << cap_bits) + (ids & (capacity - 1))
 
 
@@ -394,13 +394,11 @@
     members = n_hst * chips
 
     def places(back):
-        return [[member(h, x, n_hst, chips, back) for x in range(chips)] for h in range(n_hst)]
+        order = chip_order(n_hst, chips, back)
+        return [[order.index(h * chips + x) for x in range(chips)] for h in range(n_hst)]
 
     def exchange(blocks, back):
-        order = [0] * members
-        for host, row in enumerate(places(back)):
-            for chip, place in enumerate(row):
-                order[place] = host * chips + chip
+        order = chip_order(n_hst, chips, back)
         blocks = blocks.reshape(members, capacity, width)
         return lax.all_to_all(
             blocks, ("hst", "x"), split_axis=0, concat_axis=0, axis_index_groups=[order], tiled=True

time: 35.9 us -> 35.9 us (level)
  no operation moved by 1% of the time
where the time goes in v5:
time: 35.9 us; the launch traced here: 35.5 us
  starting transfers between devices  15.6 us (43%)
  Pallas kernels  10.4 us (29%)
  waiting for transfers between devices  8.73 us (24%)
  between operations  0.73 us (2%)
    all_to_all x2, starting transfers between devices, exchange(): lax.all_to_all(blocks, ('hst', 'x'), split_axis=0, concat_axis=0, axis_in...  15 us
    all_to_all x2, waiting for transfers between devices, exchange(): lax.all_to_all(blocks, ('hst', 'x'), split_axis=0, concat_axis=0, axis_in...  7.46 us
    pallas_call x1, Pallas kernels, update(): pl.pallas_call(update_kernel, grid=(steps,), in_specs=[pl.BlockSpec((1, s...  2.74 us
    pallas_call x2, Pallas kernels, expand(): pl.pallas_call(second_expand_kernel if last else first_expand_kernel, in_...  2.19 us
    pallas_call x2, Pallas kernels, slot_sums(): pl.pallas_call(functools.partial(sums_kernel, base=base, half=half, capac...  1.41 us
    ppermute x2, waiting for transfers between devices, swap(): return lax.ppermute(block, 'core', [(0, 1), (1, 0)])  1.27 us
    pallas_call x1, Pallas kernels, load(): pl.pallas_call(load_kernel, in_specs=[pl.BlockSpec(memory_space=pl.ANY)],...  1.22 us
    pallas_call x1, Pallas kernels, prepare(): pl.pallas_call(functools.partial(prepare_kernel, half=half, capacity=capa...  1.08 us
  transfers between devices with their start and end apart: 4, of which 4 were waited for; matrix products, arithmetic and copies ran while one was open for 0% of the time, Pallas kernels for 15%

profile of v5, /device:TPU:0, one launch (start us, length us, event | category | flops | bytes accessed | tf_op | source)
XLA Modules:
  0.0 35.5 jit_solution(371800720819971996)
XLA Ops:
  0.6 0.0 copy-start.2
  0.6 1.2 %load.1.grads_ref = bf16[2048,256]{1,0:T(8,128)(2,1)S(1)} custom-call(bf16[2048,256]{1,0:T(8,128)(2,1)} %grads_ref.1), custom_call_target="tpu_custom_call" | custom-call | bytes 2097152 | tf_op jit(solution)/shard_map/load/pallas_call | solution.py:82
  1.9 0.0 copy-done.2
  1.9 0.7 %slot_sums.3 = bf16[512,256]{1,0:T(8,128)(2,1)S(1)} custom-call(s32[1,2048]{1,0:T(1,128)S(1)} %bitcast.10, bf16[2048,256]{1,0:T(8,128)(2,1)S(1)} %load.1.grads_ref), custom_call_target="tpu_custom_call" | custom-call | flops 536870912 | bytes 1310720 | tf_op jit(solution)/shard_map/slot_sums/pallas_call | solution.py:107
  2.6 0.0 copy-start.3
  2.6 0.0 copy-start
  2.6 0.0 copy-start.1
  2.6 0.5 %collective-permute-start = (bf16[512,256]{1,0:T(8,128)(2,1)S(1)}, bf16[512,256]{1,0:T(8,128)(2,1)S(1)}, u32[]{:S(2)}, u32[]{:S(2)}) collective-permute-start(bf16[512,256]{1,0:T(8,128)(2,1)S(1)} %slot_sums.3), channel_id=1, source_target_pairs={{0,1},{1,0},{2,3},{3,2},{4,5},{5,4},{6,7},{7,6},{8,9},{9,8},{10,11... | collective-permute-start | bytes 786440 | tf_op jit(solution)/shard_map/ppermute | solution.py:392
  3.1 0.7 %slot_sums.2.a_ref = bf16[512,256]{1,0:T(8,128)(2,1)S(1)} custom-call(s32[1,2048]{1,0:T(1,128)S(1)} %bitcast.11, bf16[2048,256]{1,0:T(8,128)(2,1)S(1)} %load.1.grads_ref), custom_call_target="tpu_custom_call" | custom-call | flops 536870912 | bytes 1310720 | tf_op jit(solution)/shard_map/slot_sums/pallas_call | solution.py:107
  3.9 0.5 %collective-permute-done.b_ref = bf16[512,256]{1,0:T(8,128)(2,1)S(1)} collective-permute-done((bf16[512,256]{1,0:T(8,128)(2,1)S(1)}, bf16[512,256]{1,0:T(8,128)(2,1)S(1)}, u32[]{:S(2)}, u32[]{:S(2)}) %collective-permute-start) | collective-permute-done | bytes 262176 | tf_op jit(solution)/shard_map/ppermute | solution.py:392
  4.3 0.7 %add.1 = bf16[512,256]{1,0:T(8,128)(2,1)} custom-call(bf16[512,256]{1,0:T(8,128)(2,1)S(1)} %slot_sums.2.a_ref, bf16[512,256]{1,0:T(8,128)(2,1)S(1)} %collective-permute-done.b_ref), custom_call_target="tpu_custom_call" | custom-call | flops 131072 | bytes 786432 | tf_op jit(solution)/shard_map/add/pallas_call | solution.py:145
  5.1 8.7 %all-to-all-start = ((bf16[16,32,256]{2,1,0:T(8,128)(2,1)}), bf16[16,32,256]{2,1,0:T(8,128)(2,1)S(1)}, u32[]{:S(2)}, u32[]{:S(2)}) async-start(bf16[16,32,256]{2,1,0:T(8,128)(2,1)} %bitcast.1), calls=%async_computation | async-start | bytes 524288 | tf_op jit(solution)/shard_map/all_to_all | solution.py:403
  13.8 0.0 copy-done.3
  13.8 0.1 reshape.29.rows_ref
  13.9 1.1 %prepare.1 = (f32[256,256]{1,0:T(8,128)S(1)}, f32[256,128]{1,0:T(8,128)S(1)}, bf16[256,256]{1,0:T(8,128)(2,1)S(1)}, s16[2048,128]{1,0:T(8,128)(2,1)S(1)}) custom-call(s32[1,256]{1,0:T(1,128)S(1)} %reshape.29.rows_ref, f32[2048,256]{1,0:T(8,128)S(1)} %copy-done, f32[16,128]{1,0:T(8,128)S(1)} %bitcast.8, s32[1,2048]{1,0:T(1,128)S(1)} %bitcast.12), custom_call_target="tpu_custom_call" | custom-call | flops 536870912 | bytes 2097152 | tf_op jit(solution)/shard_map/prepare/pallas_call | solution.py:198
  15.0 5.6 %all-to-all-done.arrived_ref = bf16[16,32,256]{2,1,0:T(8,128)(2,1)S(1)} async-done(((bf16[16,32,256]{2,1,0:T(8,128)(2,1)}), bf16[16,32,256]{2,1,0:T(8,128)(2,1)S(1)}, u32[]{:S(2)}, u32[]{:S(2)}) %all-to-all-start) | async-done | bytes 262176 | tf_op jit(solution)/shard_map/all_to_all | solution.py:403
  20.6 1.0 %pick.1 = (bf16[16,32,256]{2,1,0:T(8,128)(2,1)}, bf16[256,256]{1,0:T(8,128)(2,1)S(1)}) custom-call(bf16[16,32,256]{2,1,0:T(8,128)(2,1)S(1)} %all-to-all-done.arrived_ref, f32[256,256]{1,0:T(8,128)S(1)} %get-tuple-element.14.old_ref, f32[256,128]{1,0:T(8,128)S(1)} %get-tuple-element.15.acc_ref, bf16[256,256]{1,0:T(8,128)(2,1)S(1)} %get-tuple-element.16.same_ref), custom_call_target="tpu_custom_call" | custom-call | flops 33554432 | bytes 524288 | tf_op jit(solution)/shard_map/pick/pallas_call | solution.py:248
  21.6 6.3 %all-to-all-start.1 = ((bf16[16,32,256]{2,1,0:T(8,128)(2,1)}), bf16[16,32,256]{2,1,0:T(8,128)(2,1)S(1)}, u32[]{:S(2)}, u32[]{:S(2)}) async-start(bf16[16,32,256]{2,1,0:T(8,128)(2,1)} %get-tuple-element.17), calls=%async_computation.1 | async-start | bytes 524288 | tf_op jit(solution)/shard_map/all_to_all | solution.py:403
  27.9 2.7 %update.1 = (f32[2048,256]{1,0:T(8,128)}, f32[4,4,128]{2,1,0:T(4,128)}) custom-call(s32[1,256]{1,0:T(1,128)S(1)} %reshape.29.rows_ref, bf16[256,256]{1,0:T(8,128)(2,1)S(1)} %get-tuple-element.18.sums_ref, f32[2048,256]{1,0:T(8,128)S(1)} %copy-done, f32[4,4,128]{2,1,0:T(4,128)S(1)} %bitcast.9), custom_call_target="tpu_custom_call" | custom-call | flops 268435456 | bytes 4194304 | tf_op jit(solution)/shard_map/update/pallas_call | solution.py:298
  30.7 1.8 %all-to-all-done.1 = bf16[16,32,256]{2,1,0:T(8,128)(2,1)S(1)} async-done(((bf16[16,32,256]{2,1,0:T(8,128)(2,1)}), bf16[16,32,256]{2,1,0:T(8,128)(2,1)S(1)}, u32[]{:S(2)}, u32[]{:S(2)}) %all-to-all-start.1) | async-done | bytes 262176 | tf_op jit(solution)/shard_map/all_to_all | solution.py:403
  32.5 0.0 collective-permute-start.1
  32.5 0.7 %first_expand.1.before_ref = bf16[2048,256]{1,0:T(8,128)(2,1)S(1)} custom-call(s16[2048,128]{1,0:T(8,128)(2,1)S(1)} %get-tuple-element.23.cols_ref, bf16[512,256]{1,0:T(8,128)(2,1)S(1)} %bitcast.7), custom_call_target="tpu_custom_call" | custom-call | flops 536870912 | bytes 1310720 | tf_op jit(solution)/shard_map/first_expand/pallas_call | solution.py:363
  33.2 0.8 %collective-permute-done.1.cache_ref = bf16[512,256]{1,0:T(8,128)(2,1)S(1)} collective-permute-done((bf16[512,256]{1,0:T(8,128)(2,1)S(1)}, bf16[512,256]{1,0:T(8,128)(2,1)S(1)}, u32[]{:S(2)}, u32[]{:S(2)}) %collective-permute-start.1) | collective-permute-done | bytes 262176 | tf_op jit(solution)/shard_map/ppermute | solution.py:392
  34.0 1.5 %second_expand.1 = bf16[2048,256]{1,0:T(8,128)(2,1)} custom-call(s16[2048,128]{1,0:T(8,128)(2,1)S(1)} %get-tuple-element.23.cols_ref, bf16[512,256]{1,0:T(8,128)(2,1)S(1)} %collective-permute-done.1.cache_ref, bf16[2048,256]{1,0:T(8,128)(2,1)S(1)} %first_expand.1.before_ref), custom_call_target="tpu_custom_call" | custom-call | flops 536870912 | bytes 1310720 | tf_op jit(solution)/shard_map/second_expand/pallas_call | solution.py:363
  (2 shorter events, 0.0 us)
Async XLA Ops:
  0.6 1.2 %copy-start.2 = (s32[2048]{0:T(1024)S(1)}, s32[2048]{0:T(1024)}, u32[]{:S(2)}) copy-start(s32[2048]{0:T(1024)} %param.8) | copy-start | bytes 24580
  2.6 11.2 %copy-start.3 = (s32[1,8,32]{2,1,0:T(8,128)S(1)}, s32[1,8,32]{2,1,0:T(8,128)}, u32[]{:S(2)}) copy-start(s32[1,8,32]{2,1,0:T(8,128)} %param.9) | copy-start | bytes 3076
  2.6 11.3 %copy-start = (f32[2048,256]{1,0:T(8,128)S(1)}, f32[2048,256]{1,0:T(8,128)}, u32[]{:S(2)}) copy-start(f32[2048,256]{1,0:T(8,128)} %emb_ref.3) | copy-start | bytes 6291460
  2.6 11.3 %copy-start.1 = (f32[2048]{0:T(1024)S(1)}, f32[2048]{0:T(1024)}, u32[]{:S(2)}) copy-start(f32[2048]{0:T(1024)} %param.6) | copy-start | bytes 24580
  2.6 1.7 %collective-permute-start = (bf16[512,256]{1,0:T(8,128)(2,1)S(1)}, bf16[512,256]{1,0:T(8,128)(2,1)S(1)}, u32[]{:S(2)}, u32[]{:S(2)}) collective-permute-start(bf16[512,256]{1,0:T(8,128)(2,1)S(1)} %slot_sums.3), channel_id=1, source_target_pairs={{0,1},{1,0},{2,3},{3,2},{4,5},{5,4},{6,7},{7,6},{8,9},{9,8},{10,11... | collective-permute-start | bytes 786440 | tf_op jit(solution)/shard_map/ppermute | solution.py:392
  5.1 15.5 %all-to-all-start = ((bf16[16,32,256]{2,1,0:T(8,128)(2,1)}), bf16[16,32,256]{2,1,0:T(8,128)(2,1)S(1)}, u32[]{:S(2)}, u32[]{:S(2)}) async-start(bf16[16,32,256]{2,1,0:T(8,128)(2,1)} %bitcast.1), calls=%async_computation | async-start | bytes 524288 | tf_op jit(solution)/shard_map/all_to_all | solution.py:403
  21.6 10.9 %all-to-all-start.1 = ((bf16[16,32,256]{2,1,0:T(8,128)(2,1)}), bf16[16,32,256]{2,1,0:T(8,128)(2,1)S(1)}, u32[]{:S(2)}, u32[]{:S(2)}) async-start(bf16[16,32,256]{2,1,0:T(8,128)(2,1)} %get-tuple-element.17), calls=%async_computation.1 | async-start | bytes 524288 | tf_op jit(solution)/shard_map/all_to_all | solution.py:403
  32.5 1.5 %collective-permute-start.1 = (bf16[512,256]{1,0:T(8,128)(2,1)S(1)}, bf16[512,256]{1,0:T(8,128)(2,1)S(1)}, u32[]{:S(2)}, u32[]{:S(2)}) collective-permute-start(bf16[512,256]{1,0:T(8,128)(2,1)S(1)} %bitcast.6), channel_id=1, source_target_pairs={{0,1},{1,0},{2,3},{3,2},{4,5},{5,4},{6,7},{7,6},{8,9},{9,8},{10,11... | collective-permute-start | bytes 786440 | tf_op jit(solution)/shard_map/ppermute | solution.py:392

commit v6 on v5

--- a/solution.py
+++ b/solution.py
@@ -20,25 +20,29 @@
     return 1 << (bits_of(n_hst) // 2)
 
 
-def chip_order(n_hst, chips, back):
+def chip_order(n_hst, chips, back, core):
     n_y = planes(n_hst)
     n_z, n_yx = n_hst // n_y, n_y * chips
     mid = n_z // 2
+    flip = n_yx - 1 if core and not back else 0
     if back:
         zs = [(mid + step) % n_z for step in range(n_z)]
         yxs = [*reversed(range(1, n_yx, 2)), *reversed(range(0, n_yx, 2))]
-        return [z * n_yx + yx for z in zs for yx in yxs]
+        return [z * n_yx + (yx ^ flip) for z in zs for yx in yxs]
     zs = [(mid - step) % n_z for step in range(n_z)]
     yxs = [*range(n_yx // 2, n_yx), *reversed(range(n_yx // 2))]
-    return [z * n_yx + yx for yx in yxs for z in zs]
+    return [z * n_yx + (yx ^ flip) for yx in yxs for z in zs]
 
 
 def slot_place(ids, capacity, half, back):
     cap_bits = bits_of(capacity)
-    other = ((ids >> cap_bits) & 1) ^ lax.axis_index("core")
+    core = (ids >> cap_bits) & 1
+    other = core ^ lax.axis_index("core")
     chip = ids >> (cap_bits + 1)
     place = jnp.zeros_like(chip)
-    for at, member in enumerate(chip_order(lax.axis_size("hst"), lax.axis_size("x"), back)):
+    orders = [chip_order(lax.axis_size("hst"), lax.axis_size("x"), back, c) for c in range(2)]
+    for member in range(len(orders[0])):
+        at = jnp.where(core == 0, orders[0].index(member), orders[1].index(member))
         place = jnp.where(chip == member, at, place)
     return other * half + (place << cap_bits) + (ids & (capacity - 1))
 
@@ -215,7 +219,17 @@
     )(rows, embedding, row_accum.reshape(rows_dev // 128, 128), ids)
 
 
-def pick_kernel(arrived_ref, old_ref, acc_ref, same_ref, back_ref, sums_ref, lines, sems, *, places, back_places):
+def pick_kernel(*refs, places, back_places):
+    for core in range(2):
+
+        @pl.when(lax.axis_index("core") == core)
+        def _():
+            pick_rows(*refs, places[core], back_places[core])
+
+
+def pick_rows(
+    arrived_ref, old_ref, acc_ref, same_ref, back_ref, sums_ref, lines, sems, places, back_places
+):
     capacity, width = arrived_ref.shape[1:]
     for host, members in enumerate(places):
         total = arrived_ref[members[0]].astype(jnp.float32)
@@ -243,7 +257,7 @@
 
 def pick(arrived, old, old_acc, same, places, back_places):
     _, capacity, width = arrived.shape
-    slots = len(places) * capacity
+    slots = len(places[0]) * capacity
     vmem = pl.BlockSpec(memory_space=pltpu.VMEM)
     return pl.pallas_call(
         functools.partial(pick_kernel, places=places, back_places=back_places),
@@ -393,15 +407,25 @@
 
     members = n_hst * chips
 
+    def orders(back):
+        return [chip_order(n_hst, chips, back, core) for core in range(2)]
+
     def places(back):
-        order = chip_order(n_hst, chips, back)
-        return [[order.index(h * chips + x) for x in range(chips)] for h in range(n_hst)]
+        return [
+            [[order.index(h * chips + x) for x in range(chips)] for h in range(n_hst)]
+            for order in orders(back)
+        ]
 
     def exchange(blocks, back):
-        order = chip_order(n_hst, chips, back)
+        groups = [[2 * chip + core for chip in order] for core, order in enumerate(orders(back))]
         blocks = blocks.reshape(members, capacity, width)
         return lax.all_to_all(
-            blocks, ("hst", "x"), split_axis=0, concat_axis=0, axis_index_groups=[order], tiled=True
+            blocks,
+            ("hst", "x", "core"),
+            split_axis=0,
+            concat_axis=0,
+            axis_index_groups=groups,
+            tiled=True,
         )
 
     rows = owner_rows.reshape(1, n_hst * capacity)

time: 35.9 us -> 37.6 us (1.047)
  waiting for transfers between devices: 8.73 us -> 10.5 us
    all_to_all x2, waiting for transfers between devices: 7.46 us -> 9.28 us  [exchange(): lax.all_to_all(blocks, ('hst', 'x', 'core'), split_axis=0, concat_axis=0,...]
  transfers between devices with their start and end apart: 4 -> 4, of which waited for: 4 -> 4; matrix products, arithmetic and copies ran while one was open for 0% -> 0% of each run, Pallas kernels for 15% -> 14%
where the time goes in v6:
time: 37.6 us; the launch traced here: 37.3 us
  starting transfers between devices  15.5 us (41%)
  waiting for transfers between devices  10.5 us (28%)
  Pallas kernels  10.4 us (28%)
  between operations  0.73 us (2%)
    all_to_all x2, starting transfers between devices, exchange(): lax.all_to_all(blocks, ('hst', 'x', 'core'), split_axis=0, concat_axis=0,...  14.9 us
    all_to_all x2, waiting for transfers between devices, exchange(): lax.all_to_all(blocks, ('hst', 'x', 'core'), split_axis=0, concat_axis=0,...  9.28 us
    pallas_call x1, Pallas kernels, update(): pl.pallas_call(update_kernel, grid=(steps,), in_specs=[pl.BlockSpec((1, s...  2.75 us
    pallas_call x2, Pallas kernels, expand(): pl.pallas_call(second_expand_kernel if last else first_expand_kernel, in_...  2.19 us
    pallas_call x2, Pallas kernels, slot_sums(): pl.pallas_call(functools.partial(sums_kernel, base=base, half=half, capac...  1.43 us
    ppermute x2, waiting for transfers between devices, swap(): return lax.ppermute(block, 'core', [(0, 1), (1, 0)])  1.26 us
    pallas_call x1, Pallas kernels, load(): pl.pallas_call(load_kernel, in_specs=[pl.BlockSpec(memory_space=pl.ANY)],...  1.22 us
    pallas_call x1, Pallas kernels, prepare(): pl.pallas_call(functools.partial(prepare_kernel, half=half, capacity=capa...  1.08 us
  transfers between devices with their start and end apart: 4, of which 4 were waited for; matrix products, arithmetic and copies ran while one was open for 0% of the time, Pallas kernels for 14%

profile of v6, /device:TPU:0, one launch (start us, length us, event | category | flops | bytes accessed | tf_op | source)
XLA Modules:
  0.0 37.3 jit_solution(1235152296859911536)
XLA Ops:
  0.6 1.2 %load.1.grads_ref = bf16[2048,256]{1,0:T(8,128)(2,1)S(1)} custom-call(bf16[2048,256]{1,0:T(8,128)(2,1)} %grads_ref.1), custom_call_target="tpu_custom_call" | custom-call | bytes 2097152 | tf_op jit(solution)/shard_map/load/pallas_call | solution.py:86
  1.9 0.0 copy-done.2
  1.9 0.7 %slot_sums.3 = bf16[512,256]{1,0:T(8,128)(2,1)S(1)} custom-call(s32[1,2048]{1,0:T(1,128)S(1)} %bitcast.10, bf16[2048,256]{1,0:T(8,128)(2,1)S(1)} %load.1.grads_ref), custom_call_target="tpu_custom_call" | custom-call | flops 536870912 | bytes 1310720 | tf_op jit(solution)/shard_map/slot_sums/pallas_call | solution.py:111
  2.6 0.0 copy-start.3
  2.6 0.0 copy-start
  2.6 0.0 copy-start.1
  2.6 0.5 %collective-permute-start = (bf16[512,256]{1,0:T(8,128)(2,1)S(1)}, bf16[512,256]{1,0:T(8,128)(2,1)S(1)}, u32[]{:S(2)}, u32[]{:S(2)}) collective-permute-start(bf16[512,256]{1,0:T(8,128)(2,1)S(1)} %slot_sums.3), channel_id=1, source_target_pairs={{0,1},{1,0},{2,3},{3,2},{4,5},{5,4},{6,7},{7,6},{8,9},{9,8},{10,11... | collective-permute-start | bytes 786440 | tf_op jit(solution)/shard_map/ppermute | solution.py:406
  3.2 0.7 %slot_sums.2.a_ref = bf16[512,256]{1,0:T(8,128)(2,1)S(1)} custom-call(s32[1,2048]{1,0:T(1,128)S(1)} %bitcast.11, bf16[2048,256]{1,0:T(8,128)(2,1)S(1)} %load.1.grads_ref), custom_call_target="tpu_custom_call" | custom-call | flops 536870912 | bytes 1310720 | tf_op jit(solution)/shard_map/slot_sums/pallas_call | solution.py:111
  3.9 0.4 %collective-permute-done.b_ref = bf16[512,256]{1,0:T(8,128)(2,1)S(1)} collective-permute-done((bf16[512,256]{1,0:T(8,128)(2,1)S(1)}, bf16[512,256]{1,0:T(8,128)(2,1)S(1)}, u32[]{:S(2)}, u32[]{:S(2)}) %collective-permute-start) | collective-permute-done | bytes 262176 | tf_op jit(solution)/shard_map/ppermute | solution.py:406
  4.3 0.7 %add.1 = bf16[512,256]{1,0:T(8,128)(2,1)} custom-call(bf16[512,256]{1,0:T(8,128)(2,1)S(1)} %slot_sums.2.a_ref, bf16[512,256]{1,0:T(8,128)(2,1)S(1)} %collective-permute-done.b_ref), custom_call_target="tpu_custom_call" | custom-call | flops 131072 | bytes 786432 | tf_op jit(solution)/shard_map/add/pallas_call | solution.py:149
  5.1 8.7 %all-to-all-start = ((bf16[16,32,256]{2,1,0:T(8,128)(2,1)}), bf16[16,32,256]{2,1,0:T(8,128)(2,1)S(1)}, u32[]{:S(2)}, u32[]{:S(2)}) async-start(bf16[16,32,256]{2,1,0:T(8,128)(2,1)} %bitcast.1), calls=%async_computation | async-start | bytes 524288 | tf_op jit(solution)/shard_map/all_to_all | solution.py:422
  13.8 0.0 copy-done.3
  13.8 0.1 reshape.29.rows_ref
  13.9 0.0 copy-done.1
  13.9 1.1 %prepare.1 = (f32[256,256]{1,0:T(8,128)S(1)}, f32[256,128]{1,0:T(8,128)S(1)}, bf16[256,256]{1,0:T(8,128)(2,1)S(1)}, s16[2048,128]{1,0:T(8,128)(2,1)S(1)}) custom-call(s32[1,256]{1,0:T(1,128)S(1)} %reshape.29.rows_ref, f32[2048,256]{1,0:T(8,128)S(1)} %copy-done, f32[16,128]{1,0:T(8,128)S(1)} %bitcast.8, s32[1,2048]{1,0:T(1,128)S(1)} %bitcast.12), custom_call_target="tpu_custom_call" | custom-call | flops 536870912 | bytes 2097152 | tf_op jit(solution)/shard_map/prepare/pallas_call | solution.py:202
  15.0 5.6 %all-to-all-done.refs_0_ = bf16[16,32,256]{2,1,0:T(8,128)(2,1)S(1)} async-done(((bf16[16,32,256]{2,1,0:T(8,128)(2,1)}), bf16[16,32,256]{2,1,0:T(8,128)(2,1)S(1)}, u32[]{:S(2)}, u32[]{:S(2)}) %all-to-all-start) | async-done | bytes 262176 | tf_op jit(solution)/shard_map/all_to_all | solution.py:422
  20.6 1.0 %pick.1 = (bf16[16,32,256]{2,1,0:T(8,128)(2,1)}, bf16[256,256]{1,0:T(8,128)(2,1)S(1)}) custom-call(bf16[16,32,256]{2,1,0:T(8,128)(2,1)S(1)} %all-to-all-done.refs_0_, f32[256,256]{1,0:T(8,128)S(1)} %get-tuple-element.14.refs_1_, f32[256,128]{1,0:T(8,128)S(1)} %get-tuple-element.15.refs_2_, bf16[256,256]{1,0:T(8,128)(2,1)S(1)} %get-tuple-element.16.refs_3_), custom_call_target="tpu_custom_call" | custom-call | flops 33554432 | bytes 524288 | tf_op jit(solution)/shard_map/pick/pallas_call | solution.py:262
  21.6 6.2 %all-to-all-start.1 = ((bf16[16,32,256]{2,1,0:T(8,128)(2,1)}), bf16[16,32,256]{2,1,0:T(8,128)(2,1)S(1)}, u32[]{:S(2)}, u32[]{:S(2)}) async-start(bf16[16,32,256]{2,1,0:T(8,128)(2,1)} %get-tuple-element.17), calls=%async_computation.1 | async-start | bytes 524288 | tf_op jit(solution)/shard_map/all_to_all | solution.py:422
  27.8 2.7 %update.1 = (f32[2048,256]{1,0:T(8,128)}, f32[4,4,128]{2,1,0:T(4,128)}) custom-call(s32[1,256]{1,0:T(1,128)S(1)} %reshape.29.rows_ref, bf16[256,256]{1,0:T(8,128)(2,1)S(1)} %get-tuple-element.18.sums_ref, f32[2048,256]{1,0:T(8,128)S(1)} %copy-done, f32[4,4,128]{2,1,0:T(4,128)S(1)} %bitcast.9), custom_call_target="tpu_custom_call" | custom-call | flops 268435456 | bytes 4194304 | tf_op jit(solution)/shard_map/update/pallas_call | solution.py:312
  30.6 3.7 %all-to-all-done.1 = bf16[16,32,256]{2,1,0:T(8,128)(2,1)S(1)} async-done(((bf16[16,32,256]{2,1,0:T(8,128)(2,1)}), bf16[16,32,256]{2,1,0:T(8,128)(2,1)S(1)}, u32[]{:S(2)}, u32[]{:S(2)}) %all-to-all-start.1) | async-done | bytes 262176 | tf_op jit(solution)/shard_map/all_to_all | solution.py:422
  34.2 0.0 collective-permute-start.1
  34.2 0.7 %first_expand.1.before_ref = bf16[2048,256]{1,0:T(8,128)(2,1)S(1)} custom-call(s16[2048,128]{1,0:T(8,128)(2,1)S(1)} %get-tuple-element.23.cols_ref, bf16[512,256]{1,0:T(8,128)(2,1)S(1)} %bitcast.7), custom_call_target="tpu_custom_call" | custom-call | flops 536870912 | bytes 1310720 | tf_op jit(solution)/shard_map/first_expand/pallas_call | solution.py:377
  34.9 0.8 %collective-permute-done.1.cache_ref = bf16[512,256]{1,0:T(8,128)(2,1)S(1)} collective-permute-done((bf16[512,256]{1,0:T(8,128)(2,1)S(1)}, bf16[512,256]{1,0:T(8,128)(2,1)S(1)}, u32[]{:S(2)}, u32[]{:S(2)}) %collective-permute-start.1) | collective-permute-done | bytes 262176 | tf_op jit(solution)/shard_map/ppermute | solution.py:406
  35.8 1.5 %second_expand.1 = bf16[2048,256]{1,0:T(8,128)(2,1)} custom-call(s16[2048,128]{1,0:T(8,128)(2,1)S(1)} %get-tuple-element.23.cols_ref, bf16[512,256]{1,0:T(8,128)(2,1)S(1)} %collective-permute-done.1.cache_ref, bf16[2048,256]{1,0:T(8,128)(2,1)S(1)} %first_expand.1.before_ref), custom_call_target="tpu_custom_call" | custom-call | flops 536870912 | bytes 1310720 | tf_op jit(solution)/shard_map/second_expand/pallas_call | solution.py:377
  (2 shorter events, 0.0 us)
Async XLA Ops:
  0.6 1.2 %copy-start.2 = (s32[2048]{0:T(1024)S(1)}, s32[2048]{0:T(1024)}, u32[]{:S(2)}) copy-start(s32[2048]{0:T(1024)} %param.8) | copy-start | bytes 24580
  2.6 11.2 %copy-start.3 = (s32[1,8,32]{2,1,0:T(8,128)S(1)}, s32[1,8,32]{2,1,0:T(8,128)}, u32[]{:S(2)}) copy-start(s32[1,8,32]{2,1,0:T(8,128)} %param.9) | copy-start | bytes 3076
  2.6 11.3 %copy-start = (f32[2048,256]{1,0:T(8,128)S(1)}, f32[2048,256]{1,0:T(8,128)}, u32[]{:S(2)}) copy-start(f32[2048,256]{1,0:T(8,128)} %emb_ref.3) | copy-start | bytes 6291460
  2.6 11.3 %copy-start.1 = (f32[2048]{0:T(1024)S(1)}, f32[2048]{0:T(1024)}, u32[]{:S(2)}) copy-start(f32[2048]{0:T(1024)} %param.6) | copy-start | bytes 24580
  2.6 1.7 %collective-permute-start = (bf16[512,256]{1,0:T(8,128)(2,1)S(1)}, bf16[512,256]{1,0:T(8,128)(2,1)S(1)}, u32[]{:S(2)}, u32[]{:S(2)}) collective-permute-start(bf16[512,256]{1,0:T(8,128)(2,1)S(1)} %slot_sums.3), channel_id=1, source_target_pairs={{0,1},{1,0},{2,3},{3,2},{4,5},{5,4},{6,7},{7,6},{8,9},{9,8},{10,11... | collective-permute-start | bytes 786440 | tf_op jit(solution)/shard_map/ppermute | solution.py:406
  5.1 15.5 %all-to-all-start = ((bf16[16,32,256]{2,1,0:T(8,128)(2,1)}), bf16[16,32,256]{2,1,0:T(8,128)(2,1)S(1)}, u32[]{:S(2)}, u32[]{:S(2)}) async-start(bf16[16,32,256]{2,1,0:T(8,128)(2,1)} %bitcast.1), calls=%async_computation | async-start | bytes 524288 | tf_op jit(solution)/shard_map/all_to_all | solution.py:422
  21.6 12.6 %all-to-all-start.1 = ((bf16[16,32,256]{2,1,0:T(8,128)(2,1)}), bf16[16,32,256]{2,1,0:T(8,128)(2,1)S(1)}, u32[]{:S(2)}, u32[]{:S(2)}) async-start(bf16[16,32,256]{2,1,0:T(8,128)(2,1)} %get-tuple-element.17), calls=%async_computation.1 | async-start | bytes 524288 | tf_op jit(solution)/shard_map/all_to_all | solution.py:422
  34.2 1.5 %collective-permute-start.1 = (bf16[512,256]{1,0:T(8,128)(2,1)S(1)}, bf16[512,256]{1,0:T(8,128)(2,1)S(1)}, u32[]{:S(2)}, u32[]{:S(2)}) collective-permute-start(bf16[512,256]{1,0:T(8,128)(2,1)S(1)} %bitcast.6), channel_id=1, source_target_pairs={{0,1},{1,0},{2,3},{3,2},{4,5},{5,4},{6,7},{7,6},{8,9},{9,8},{10,11... | collective-permute-start | bytes 786440 | tf_op jit(solution)/shard_map/ppermute | solution.py:406

commit v7 on v4

--- a/solution.py
+++ b/solution.py
@@ -320,32 +320,56 @@
     return new_emb, new_acc.reshape(rows_dev)
 
 
-def chosen_rows(cols, cache, base):
-    lookups = cols.shape[0]
+def chosen(cols, slots, base):
     lane = lax.broadcasted_iota(jnp.int32, (16, 128), 1)
     tiles = []
-    for start in range(0, cache.shape[0], 128):
+    for start in range(0, slots, 128):
         here = small(lane + (base + start))
-        tiles.append(matches(cols, jnp.concatenate([here] * (lookups // 16), axis=0)))
-    return jnp.dot(
-        jnp.concatenate(tiles, axis=1), cache, preferred_element_type=jnp.float32
-    ).astype(jnp.bfloat16)
-
-
-def first_expand_kernel(cols_ref, cache_ref, out_ref):
-    block = min(1024, MIB // cache_ref.shape[0])
+        tiles.append(matches(cols, jnp.concatenate([here] * (cols.shape[0] // 16), axis=0)))
+    return jnp.concatenate(tiles, axis=1)
+
+
+def product(onehot, cache):
+    return jnp.dot(onehot, cache, preferred_element_type=jnp.float32).astype(jnp.bfloat16)
+
+
+def first_expand_kernel(cols_ref, cache_ref, out_ref, other_ref):
+    slots = cache_ref.shape[0]
+    block = min(1024, MIB // slots)
     for start in range(0, out_ref.shape[0], block):
         at = slice(start, start + block)
-        out_ref[at, :] = chosen_rows(cols_ref[at, :], cache_ref[...], 0)
-
-
-def second_expand_kernel(cols_ref, cache_ref, before_ref, out_ref, lines, sems):
+        out_ref[at, :] = product(chosen(cols_ref[at, :], slots, 0), cache_ref[...])
+        other_ref[at, :] = chosen(cols_ref[at, :], slots, slots)
+
+
+def first_expand(cols, cache):
+    slots, width = cache.shape
+    tokens = cols.shape[0]
+    vmem = pl.BlockSpec(memory_space=pltpu.VMEM)
+    return pl.pallas_call(
+        first_expand_kernel,
+        in_specs=[vmem] * 2,
+        out_specs=[vmem] * 2,
+        out_shape=[
+            jax.ShapeDtypeStruct((tokens, width), jnp.bfloat16),
+            jax.ShapeDtypeStruct((tokens, slots), jnp.bfloat16),
+        ],
+        compiler_params=pltpu.CompilerParams(vmem_limit_bytes=40 * MIB),
+        cost_estimate=pl.CostEstimate(
+            flops=2 * slots * tokens * width,
+            bytes_accessed=2 * tokens * (width + slots),
+            transcendentals=0,
+        ),
+        name="first_expand",
+    )(cols, cache)
+
+
+def second_expand_kernel(onehot_ref, cache_ref, before_ref, out_ref, lines, sems):
     block = lines.shape[0] // sems.shape[0]
     copies = []
     for start in range(0, lines.shape[0], block):
         at = slice(start, start + block)
-        rows = chosen_rows(cols_ref[at, :], cache_ref[...], cache_ref.shape[0])
-        lines[at, :] = rows + before_ref[at, :]
+        lines[at, :] = product(onehot_ref[at, :], cache_ref[...]) + before_ref[at, :]
         window = pl.ds(start, block)
         copies.append(
             pltpu.make_async_copy(lines.at[window], out_ref.at[window], sems.at[start // block])
@@ -355,30 +379,27 @@
         copy.wait()
 
 
-def expand(cols, cache, before=None):
+def second_expand(onehot, cache, before):
     slots, width = cache.shape
-    tokens = cols.shape[0]
+    tokens = onehot.shape[0]
     vmem = pl.BlockSpec(memory_space=pltpu.VMEM)
-    last = before is not None
-    return pl.pallas_call(
-        second_expand_kernel if last else first_expand_kernel,
-        in_specs=[vmem] * (2 + last),
-        out_specs=pl.BlockSpec(memory_space=pltpu.HBM) if last else vmem,
+    return pl.pallas_call(
+        second_expand_kernel,
+        in_specs=[vmem] * 3,
+        out_specs=pl.BlockSpec(memory_space=pltpu.HBM),
         out_shape=jax.ShapeDtypeStruct((tokens, width), jnp.bfloat16),
         scratch_shapes=[
             pltpu.VMEM((tokens, width), jnp.bfloat16),
             pltpu.SemaphoreType.DMA((tokens // 256,)),
-        ]
-        if last
-        else [],
+        ],
         compiler_params=pltpu.CompilerParams(vmem_limit_bytes=32 * MIB),
         cost_estimate=pl.CostEstimate(
             flops=2 * slots * tokens * width,
-            bytes_accessed=2 * (tokens + slots) * width,
+            bytes_accessed=2 * tokens * (width + slots),
             transcendentals=0,
         ),
-        name="second_expand" if last else "first_expand",
-    )(cols, cache, *([before] if last else []))
+        name="second_expand",
+    )(onehot, cache, before)
 
 
 def local(embedding, row_accum, lookup_grads, lookup_slot, owner_rows):
@@ -419,8 +440,8 @@
     cache, new_embedding, new_accum = lax.optimization_barrier((cache, new_embedding, new_accum))
 
     other = swap(cache)
-    fresh_rows = expand(cols, cache)
-    fresh_rows = expand(cols, other, fresh_rows)
+    fresh_rows, onehot = first_expand(cols, cache)
+    fresh_rows = second_expand(onehot, other, fresh_rows)
     return (new_embedding, new_accum, fresh_rows)
 
 

time: 35.9 us -> 35.9 us (level)
  Pallas kernels: 10.4 us -> 11 us
  waiting for transfers between devices: 8.72 us -> 8.13 us
    ppermute x2, waiting for transfers between devices: 1.27 us -> 0.68 us  [swap(): return lax.ppermute(block, 'core', [(0, 1), (1, 0)])]
    pallas_call x2, Pallas kernels: 2.19 us -> 2.78 us  [the longest x1 1.48 us: second_expand(): pl.pallas_call(second_expand_kernel, in_specs=[vmem] * 3, out_specs=pl.Bl...]
  transfers between devices with their start and end apart: 4 -> 4, of which waited for: 4 -> 4; matrix products, arithmetic and copies ran while one was open for 0% -> 0% of each run, Pallas kernels for 15% -> 16%
where the time goes in v7:
time: 35.9 us; the launch traced here: 35.5 us
  starting transfers between devices  15.5 us (43%)
  Pallas kernels  11 us (31%)
  waiting for transfers between devices  8.13 us (23%)
  between operations  0.73 us (2%)
    all_to_all x2, starting transfers between devices, exchange(): lax.all_to_all(blocks, ('hst', 'x'), split_axis=0, concat_axis=0, axis_in...  15 us
    all_to_all x2, waiting for transfers between devices, exchange(): lax.all_to_all(blocks, ('hst', 'x'), split_axis=0, concat_axis=0, axis_in...  7.45 us
    pallas_call x1, Pallas kernels, update(): pl.pallas_call(update_kernel, grid=(steps,), in_specs=[pl.BlockSpec((1, s...  2.75 us
    pallas_call x1, Pallas kernels, second_expand(): pl.pallas_call(second_expand_kernel, in_specs=[vmem] * 3, out_specs=pl.Bl...  1.48 us
    pallas_call x2, Pallas kernels, slot_sums(): pl.pallas_call(functools.partial(sums_kernel, base=base, half=half, capac...  1.42 us
    pallas_call x1, Pallas kernels, first_expand(): pl.pallas_call(first_expand_kernel, in_specs=[vmem] * 2, out_specs=[vmem]...  1.3 us
    pallas_call x1, Pallas kernels, load(): pl.pallas_call(load_kernel, in_specs=[pl.BlockSpec(memory_space=pl.ANY)],...  1.22 us
    pallas_call x1, Pallas kernels, prepare(): pl.pallas_call(functools.partial(prepare_kernel, half=half, capacity=capa...  1.07 us
  transfers between devices with their start and end apart: 4, of which 4 were waited for; matrix products, arithmetic and copies ran while one was open for 0% of the time, Pallas kernels for 16%

profile of v7, /device:TPU:0, one launch (start us, length us, event | category | flops | bytes accessed | tf_op | source)
XLA Modules:
  0.0 35.5 jit_solution(2591115164785040323)
XLA Ops:
  0.6 0.0 copy-start.2
  0.6 1.2 %load.1.grads_ref = bf16[2048,256]{1,0:T(8,128)(2,1)S(1)} custom-call(bf16[2048,256]{1,0:T(8,128)(2,1)} %grads_ref.1), custom_call_target="tpu_custom_call" | custom-call | bytes 2097152 | tf_op jit(solution)/shard_map/load/pallas_call | solution.py:82
  1.9 0.0 copy-done.2
  1.9 0.7 %slot_sums.3 = bf16[512,256]{1,0:T(8,128)(2,1)S(1)} custom-call(s32[1,2048]{1,0:T(1,128)S(1)} %bitcast.10, bf16[2048,256]{1,0:T(8,128)(2,1)S(1)} %load.1.grads_ref), custom_call_target="tpu_custom_call" | custom-call | flops 536870912 | bytes 1310720 | tf_op jit(solution)/shard_map/slot_sums/pallas_call | solution.py:107
  2.6 0.0 copy-start.3
  2.6 0.0 copy-start
  2.6 0.0 copy-start.1
  2.6 0.5 %collective-permute-start = (bf16[512,256]{1,0:T(8,128)(2,1)S(1)}, bf16[512,256]{1,0:T(8,128)(2,1)S(1)}, u32[]{:S(2)}, u32[]{:S(2)}) collective-permute-start(bf16[512,256]{1,0:T(8,128)(2,1)S(1)} %slot_sums.3), channel_id=1, source_target_pairs={{0,1},{1,0},{2,3},{3,2},{4,5},{5,4},{6,7},{7,6},{8,9},{9,8},{10,11... | collective-permute-start | bytes 786440 | tf_op jit(solution)/shard_map/ppermute | solution.py:413
  3.1 0.7 %slot_sums.2.a_ref = bf16[512,256]{1,0:T(8,128)(2,1)S(1)} custom-call(s32[1,2048]{1,0:T(1,128)S(1)} %bitcast.11, bf16[2048,256]{1,0:T(8,128)(2,1)S(1)} %load.1.grads_ref), custom_call_target="tpu_custom_call" | custom-call | flops 536870912 | bytes 1310720 | tf_op jit(solution)/shard_map/slot_sums/pallas_call | solution.py:107
  3.9 0.4 %collective-permute-done.b_ref = bf16[512,256]{1,0:T(8,128)(2,1)S(1)} collective-permute-done((bf16[512,256]{1,0:T(8,128)(2,1)S(1)}, bf16[512,256]{1,0:T(8,128)(2,1)S(1)}, u32[]{:S(2)}, u32[]{:S(2)}) %collective-permute-start) | collective-permute-done | bytes 262176 | tf_op jit(solution)/shard_map/ppermute | solution.py:413
  4.3 0.7 %add.1 = bf16[512,256]{1,0:T(8,128)(2,1)} custom-call(bf16[512,256]{1,0:T(8,128)(2,1)S(1)} %slot_sums.2.a_ref, bf16[512,256]{1,0:T(8,128)(2,1)S(1)} %collective-permute-done.b_ref), custom_call_target="tpu_custom_call" | custom-call | flops 131072 | bytes 786432 | tf_op jit(solution)/shard_map/add/pallas_call | solution.py:145
  5.1 8.7 %all-to-all-start = ((bf16[16,32,256]{2,1,0:T(8,128)(2,1)}), bf16[16,32,256]{2,1,0:T(8,128)(2,1)S(1)}, u32[]{:S(2)}, u32[]{:S(2)}) async-start(bf16[16,32,256]{2,1,0:T(8,128)(2,1)} %bitcast.1), calls=%async_computation | async-start | bytes 524288 | tf_op jit(solution)/shard_map/all_to_all | solution.py:426
  13.8 0.1 reshape.29.rows_ref
  13.9 0.0 copy-done.1
  13.9 1.1 %prepare.1 = (f32[256,256]{1,0:T(8,128)S(1)}, f32[256,128]{1,0:T(8,128)S(1)}, bf16[256,256]{1,0:T(8,128)(2,1)S(1)}, s16[2048,128]{1,0:T(8,128)(2,1)S(1)}) custom-call(s32[1,256]{1,0:T(1,128)S(1)} %reshape.29.rows_ref, f32[2048,256]{1,0:T(8,128)S(1)} %copy-done, f32[16,128]{1,0:T(8,128)S(1)} %bitcast.8, s32[1,2048]{1,0:T(1,128)S(1)} %bitcast.12), custom_call_target="tpu_custom_call" | custom-call | flops 536870912 | bytes 2097152 | tf_op jit(solution)/shard_map/prepare/pallas_call | solution.py:198
  15.0 5.6 %all-to-all-done.arrived_ref = bf16[16,32,256]{2,1,0:T(8,128)(2,1)S(1)} async-done(((bf16[16,32,256]{2,1,0:T(8,128)(2,1)}), bf16[16,32,256]{2,1,0:T(8,128)(2,1)S(1)}, u32[]{:S(2)}, u32[]{:S(2)}) %all-to-all-start) | async-done | bytes 262176 | tf_op jit(solution)/shard_map/all_to_all | solution.py:426
  20.6 1.0 %pick.1 = (bf16[16,32,256]{2,1,0:T(8,128)(2,1)}, bf16[256,256]{1,0:T(8,128)(2,1)S(1)}) custom-call(bf16[16,32,256]{2,1,0:T(8,128)(2,1)S(1)} %all-to-all-done.arrived_ref, f32[256,256]{1,0:T(8,128)S(1)} %get-tuple-element.16.old_ref, f32[256,128]{1,0:T(8,128)S(1)} %get-tuple-element.17.acc_ref, bf16[256,256]{1,0:T(8,128)(2,1)S(1)} %get-tuple-element.18.same_ref), custom_call_target="tpu_custom_call" | custom-call | flops 33554432 | bytes 524288 | tf_op jit(solution)/shard_map/pick/pallas_call | solution.py:248
  21.6 6.3 %all-to-all-start.1 = ((bf16[16,32,256]{2,1,0:T(8,128)(2,1)}), bf16[16,32,256]{2,1,0:T(8,128)(2,1)S(1)}, u32[]{:S(2)}, u32[]{:S(2)}) async-start(bf16[16,32,256]{2,1,0:T(8,128)(2,1)} %get-tuple-element.19), calls=%async_computation.1 | async-start | bytes 524288 | tf_op jit(solution)/shard_map/all_to_all | solution.py:426
  27.9 2.7 %update.1 = (f32[2048,256]{1,0:T(8,128)}, f32[4,4,128]{2,1,0:T(4,128)}) custom-call(s32[1,256]{1,0:T(1,128)S(1)} %reshape.29.rows_ref, bf16[256,256]{1,0:T(8,128)(2,1)S(1)} %get-tuple-element.20.sums_ref, f32[2048,256]{1,0:T(8,128)S(1)} %copy-done, f32[4,4,128]{2,1,0:T(4,128)S(1)} %bitcast.9), custom_call_target="tpu_custom_call" | custom-call | flops 268435456 | bytes 4194304 | tf_op jit(solution)/shard_map/update/pallas_call | solution.py:298
  30.7 1.8 %all-to-all-done.1 = bf16[16,32,256]{2,1,0:T(8,128)(2,1)S(1)} async-done(((bf16[16,32,256]{2,1,0:T(8,128)(2,1)}), bf16[16,32,256]{2,1,0:T(8,128)(2,1)S(1)}, u32[]{:S(2)}, u32[]{:S(2)}) %all-to-all-start.1) | async-done | bytes 262176 | tf_op jit(solution)/shard_map/all_to_all | solution.py:426
  32.5 0.0 collective-permute-start.1
  32.5 1.3 %first_expand.1 = (bf16[2048,256]{1,0:T(8,128)(2,1)S(1)}, bf16[2048,512]{1,0:T(8,128)(2,1)S(1)}) custom-call(s16[2048,128]{1,0:T(8,128)(2,1)S(1)} %get-tuple-element.25.cols_ref, bf16[512,256]{1,0:T(8,128)(2,1)S(1)} %bitcast.7), custom_call_target="tpu_custom_call" | custom-call | flops 536870912 | bytes 3145728 | tf_op jit(solution)/shard_map/first_expand/pallas_call | solution.py:349
  33.8 0.2 collective-permute-done.1.cache_ref
  34.0 1.5 %second_expand.1 = bf16[2048,256]{1,0:T(8,128)(2,1)} custom-call(bf16[2048,512]{1,0:T(8,128)(2,1)S(1)} %get-tuple-element.27.onehot_ref, bf16[512,256]{1,0:T(8,128)(2,1)S(1)} %collective-permute-done.1.cache_ref, bf16[2048,256]{1,0:T(8,128)(2,1)S(1)} %get-tuple-element.28.before_ref), custom_call_target="tpu_custom_call" | custom-call | flops 536870912 | bytes 3145728 | tf_op jit(solution)/shard_map/second_expand/pallas_call | solution.py:386
  (2 shorter events, 0.0 us)
Async XLA Ops:
  0.6 1.2 %copy-start.2 = (s32[2048]{0:T(1024)S(1)}, s32[2048]{0:T(1024)}, u32[]{:S(2)}) copy-start(s32[2048]{0:T(1024)} %param.8) | copy-start | bytes 24580
  2.6 11.2 %copy-start.3 = (s32[1,8,32]{2,1,0:T(8,128)S(1)}, s32[1,8,32]{2,1,0:T(8,128)}, u32[]{:S(2)}) copy-start(s32[1,8,32]{2,1,0:T(8,128)} %param.9) | copy-start | bytes 3076
  2.6 11.3 %copy-start = (f32[2048,256]{1,0:T(8,128)S(1)}, f32[2048,256]{1,0:T(8,128)}, u32[]{:S(2)}) copy-start(f32[2048,256]{1,0:T(8,128)} %emb_ref.3) | copy-start | bytes 6291460
  2.6 11.3 %copy-start.1 = (f32[2048]{0:T(1024)S(1)}, f32[2048]{0:T(1024)}, u32[]{:S(2)}) copy-start(f32[2048]{0:T(1024)} %param.6) | copy-start | bytes 24580
  2.6 1.7 %collective-permute-start = (bf16[512,256]{1,0:T(8,128)(2,1)S(1)}, bf16[512,256]{1,0:T(8,128)(2,1)S(1)}, u32[]{:S(2)}, u32[]{:S(2)}) collective-permute-start(bf16[512,256]{1,0:T(8,128)(2,1)S(1)} %slot_sums.3), channel_id=1, source_target_pairs={{0,1},{1,0},{2,3},{3,2},{4,5},{5,4},{6,7},{7,6},{8,9},{9,8},{10,11... | collective-permute-start | bytes 786440 | tf_op jit(solution)/shard_map/ppermute | solution.py:413
  5.1 15.5 %all-to-all-start = ((bf16[16,32,256]{2,1,0:T(8,128)(2,1)}), bf16[16,32,256]{2,1,0:T(8,128)(2,1)S(1)}, u32[]{:S(2)}, u32[]{:S(2)}) async-start(bf16[16,32,256]{2,1,0:T(8,128)(2,1)} %bitcast.1), calls=%async_computation | async-start | bytes 524288 | tf_op jit(solution)/shard_map/all_to_all | solution.py:426
  21.6 10.9 %all-to-all-start.1 = ((bf16[16,32,256]{2,1,0:T(8,128)(2,1)}), bf16[16,32,256]{2,1,0:T(8,128)(2,1)S(1)}, u32[]{:S(2)}, u32[]{:S(2)}) async-start(bf16[16,32,256]{2,1,0:T(8,128)(2,1)} %get-tuple-element.19), calls=%async_computation.1 | async-start | bytes 524288 | tf_op jit(solution)/shard_map/all_to_all | solution.py:426
  32.5 1.5 %collective-permute-start.1 = (bf16[512,256]{1,0:T(8,128)(2,1)S(1)}, bf16[512,256]{1,0:T(8,128)(2,1)S(1)}, u32[]{:S(2)}, u32[]{:S(2)}) collective-permute-start(bf16[512,256]{1,0:T(8,128)(2,1)S(1)} %bitcast.6), channel_id=1, source_target_pairs={{0,1},{1,0},{2,3},{3,2},{4,5},{5,4},{6,7},{7,6},{8,9},{9,8},{10,11... | collective-permute-start | bytes 786440 | tf_op jit(solution)/shard_map/ppermute | solution.py:413

commit v8 on v5

--- a/solution.py
+++ b/solution.py
@@ -25,7 +25,7 @@
     n_z, n_yx = n_hst // n_y, n_y * chips
     mid = n_z // 2
     if back:
-        zs = [(mid + step) % n_z for step in range(n_z)]
+        zs = [*range(mid, n_z), *reversed(range(mid))]
         yxs = [*reversed(range(1, n_yx, 2)), *reversed(range(0, n_yx, 2))]
         return [z * n_yx + yx for z in zs for yx in yxs]
     zs = [(mid - step) % n_z for step in range(n_z)]

time: 35.9 us -> 36.5 us (1.017)
  waiting for transfers between devices: 8.73 us -> 9.22 us
    all_to_all x2, waiting for transfers between devices: 7.46 us -> 7.95 us  [exchange(): lax.all_to_all(blocks, ('hst', 'x'), split_axis=0, concat_axis=0, axis_in...]
where the time goes in v8:
time: 36.5 us; the launch traced here: 36.1 us
  starting transfers between devices  15.6 us (43%)
  Pallas kernels  10.4 us (28%)
  waiting for transfers between devices  9.22 us (25%)
  between operations  0.73 us (2%)
    all_to_all x2, starting transfers between devices, exchange(): lax.all_to_all(blocks, ('hst', 'x'), split_axis=0, concat_axis=0, axis_in...  15.1 us
    all_to_all x2, waiting for transfers between devices, exchange(): lax.all_to_all(blocks, ('hst', 'x'), split_axis=0, concat_axis=0, axis_in...  7.95 us
    pallas_call x1, Pallas kernels, update(): pl.pallas_call(update_kernel, grid=(steps,), in_specs=[pl.BlockSpec((1, s...  2.76 us
    pallas_call x2, Pallas kernels, expand(): pl.pallas_call(second_expand_kernel if last else first_expand_kernel, in_...  2.19 us
    pallas_call x2, Pallas kernels, slot_sums(): pl.pallas_call(functools.partial(sums_kernel, base=base, half=half, capac...  1.41 us
    ppermute x2, waiting for transfers between devices, swap(): return lax.ppermute(block, 'core', [(0, 1), (1, 0)])  1.27 us
    pallas_call x1, Pallas kernels, load(): pl.pallas_call(load_kernel, in_specs=[pl.BlockSpec(memory_space=pl.ANY)],...  1.22 us
    pallas_call x1, Pallas kernels, prepare(): pl.pallas_call(functools.partial(prepare_kernel, half=half, capacity=capa...  1.08 us
  transfers between devices with their start and end apart: 4, of which 4 were waited for; matrix products, arithmetic and copies ran while one was open for 0% of the time, Pallas kernels for 15%

profile of v8, /device:TPU:0, one launch (start us, length us, event | category | flops | bytes accessed | tf_op | source)
XLA Modules:
  0.0 36.1 jit_solution(2028345789007343958)
XLA Ops:
  0.6 0.0 copy-start.2
  0.6 1.2 %load.1.grads_ref = bf16[2048,256]{1,0:T(8,128)(2,1)S(1)} custom-call(bf16[2048,256]{1,0:T(8,128)(2,1)} %grads_ref.1), custom_call_target="tpu_custom_call" | custom-call | bytes 2097152 | tf_op jit(solution)/shard_map/load/pallas_call | solution.py:82
  1.9 0.0 copy-done.2
  1.9 0.7 %slot_sums.3 = bf16[512,256]{1,0:T(8,128)(2,1)S(1)} custom-call(s32[1,2048]{1,0:T(1,128)S(1)} %bitcast.10, bf16[2048,256]{1,0:T(8,128)(2,1)S(1)} %load.1.grads_ref), custom_call_target="tpu_custom_call" | custom-call | flops 536870912 | bytes 1310720 | tf_op jit(solution)/shard_map/slot_sums/pallas_call | solution.py:107
  2.6 0.0 copy-start.3
  2.6 0.0 copy-start
  2.6 0.0 copy-start.1
  2.6 0.5 %collective-permute-start = (bf16[512,256]{1,0:T(8,128)(2,1)S(1)}, bf16[512,256]{1,0:T(8,128)(2,1)S(1)}, u32[]{:S(2)}, u32[]{:S(2)}) collective-permute-start(bf16[512,256]{1,0:T(8,128)(2,1)S(1)} %slot_sums.3), channel_id=1, source_target_pairs={{0,1},{1,0},{2,3},{3,2},{4,5},{5,4},{6,7},{7,6},{8,9},{9,8},{10,11... | collective-permute-start | bytes 786440 | tf_op jit(solution)/shard_map/ppermute | solution.py:392
  3.1 0.7 %slot_sums.2.a_ref = bf16[512,256]{1,0:T(8,128)(2,1)S(1)} custom-call(s32[1,2048]{1,0:T(1,128)S(1)} %bitcast.11, bf16[2048,256]{1,0:T(8,128)(2,1)S(1)} %load.1.grads_ref), custom_call_target="tpu_custom_call" | custom-call | flops 536870912 | bytes 1310720 | tf_op jit(solution)/shard_map/slot_sums/pallas_call | solution.py:107
  3.9 0.5 %collective-permute-done.b_ref = bf16[512,256]{1,0:T(8,128)(2,1)S(1)} collective-permute-done((bf16[512,256]{1,0:T(8,128)(2,1)S(1)}, bf16[512,256]{1,0:T(8,128)(2,1)S(1)}, u32[]{:S(2)}, u32[]{:S(2)}) %collective-permute-start) | collective-permute-done | bytes 262176 | tf_op jit(solution)/shard_map/ppermute | solution.py:392
  4.3 0.7 %add.1 = bf16[512,256]{1,0:T(8,128)(2,1)} custom-call(bf16[512,256]{1,0:T(8,128)(2,1)S(1)} %slot_sums.2.a_ref, bf16[512,256]{1,0:T(8,128)(2,1)S(1)} %collective-permute-done.b_ref), custom_call_target="tpu_custom_call" | custom-call | flops 131072 | bytes 786432 | tf_op jit(solution)/shard_map/add/pallas_call | solution.py:145
  5.1 8.7 %all-to-all-start = ((bf16[16,32,256]{2,1,0:T(8,128)(2,1)}), bf16[16,32,256]{2,1,0:T(8,128)(2,1)S(1)}, u32[]{:S(2)}, u32[]{:S(2)}) async-start(bf16[16,32,256]{2,1,0:T(8,128)(2,1)} %bitcast.1), calls=%async_computation | async-start | bytes 524288 | tf_op jit(solution)/shard_map/all_to_all | solution.py:403
  13.8 0.0 copy-done.3
  13.8 0.1 reshape.29.rows_ref
  13.9 1.1 %prepare.1 = (f32[256,256]{1,0:T(8,128)S(1)}, f32[256,128]{1,0:T(8,128)S(1)}, bf16[256,256]{1,0:T(8,128)(2,1)S(1)}, s16[2048,128]{1,0:T(8,128)(2,1)S(1)}) custom-call(s32[1,256]{1,0:T(1,128)S(1)} %reshape.29.rows_ref, f32[2048,256]{1,0:T(8,128)S(1)} %copy-done, f32[16,128]{1,0:T(8,128)S(1)} %bitcast.8, s32[1,2048]{1,0:T(1,128)S(1)} %bitcast.12), custom_call_target="tpu_custom_call" | custom-call | flops 536870912 | bytes 2097152 | tf_op jit(solution)/shard_map/prepare/pallas_call | solution.py:198
  15.0 5.6 %all-to-all-done.arrived_ref = bf16[16,32,256]{2,1,0:T(8,128)(2,1)S(1)} async-done(((bf16[16,32,256]{2,1,0:T(8,128)(2,1)}), bf16[16,32,256]{2,1,0:T(8,128)(2,1)S(1)}, u32[]{:S(2)}, u32[]{:S(2)}) %all-to-all-start) | async-done | bytes 262176 | tf_op jit(solution)/shard_map/all_to_all | solution.py:403
  20.6 1.0 %pick.1 = (bf16[16,32,256]{2,1,0:T(8,128)(2,1)}, bf16[256,256]{1,0:T(8,128)(2,1)S(1)}) custom-call(bf16[16,32,256]{2,1,0:T(8,128)(2,1)S(1)} %all-to-all-done.arrived_ref, f32[256,256]{1,0:T(8,128)S(1)} %get-tuple-element.14.old_ref, f32[256,128]{1,0:T(8,128)S(1)} %get-tuple-element.15.acc_ref, bf16[256,256]{1,0:T(8,128)(2,1)S(1)} %get-tuple-element.16.same_ref), custom_call_target="tpu_custom_call" | custom-call | flops 33554432 | bytes 524288 | tf_op jit(solution)/shard_map/pick/pallas_call | solution.py:248
  21.6 6.3 %all-to-all-start.1 = ((bf16[16,32,256]{2,1,0:T(8,128)(2,1)}), bf16[16,32,256]{2,1,0:T(8,128)(2,1)S(1)}, u32[]{:S(2)}, u32[]{:S(2)}) async-start(bf16[16,32,256]{2,1,0:T(8,128)(2,1)} %get-tuple-element.17), calls=%async_computation.1 | async-start | bytes 524288 | tf_op jit(solution)/shard_map/all_to_all | solution.py:403
  28.0 2.8 %update.1 = (f32[2048,256]{1,0:T(8,128)}, f32[4,4,128]{2,1,0:T(4,128)}) custom-call(s32[1,256]{1,0:T(1,128)S(1)} %reshape.29.rows_ref, bf16[256,256]{1,0:T(8,128)(2,1)S(1)} %get-tuple-element.18.sums_ref, f32[2048,256]{1,0:T(8,128)S(1)} %copy-done, f32[4,4,128]{2,1,0:T(4,128)S(1)} %bitcast.9), custom_call_target="tpu_custom_call" | custom-call | flops 268435456 | bytes 4194304 | tf_op jit(solution)/shard_map/update/pallas_call | solution.py:298
  30.7 2.3 %all-to-all-done.1 = bf16[16,32,256]{2,1,0:T(8,128)(2,1)S(1)} async-done(((bf16[16,32,256]{2,1,0:T(8,128)(2,1)}), bf16[16,32,256]{2,1,0:T(8,128)(2,1)S(1)}, u32[]{:S(2)}, u32[]{:S(2)}) %all-to-all-start.1) | async-done | bytes 262176 | tf_op jit(solution)/shard_map/all_to_all | solution.py:403
  33.0 0.0 collective-permute-start.1
  33.0 0.7 %first_expand.1.before_ref = bf16[2048,256]{1,0:T(8,128)(2,1)S(1)} custom-call(s16[2048,128]{1,0:T(8,128)(2,1)S(1)} %get-tuple-element.23.cols_ref, bf16[512,256]{1,0:T(8,128)(2,1)S(1)} %bitcast.7), custom_call_target="tpu_custom_call" | custom-call | flops 536870912 | bytes 1310720 | tf_op jit(solution)/shard_map/first_expand/pallas_call | solution.py:363
  33.7 0.8 %collective-permute-done.1.cache_ref = bf16[512,256]{1,0:T(8,128)(2,1)S(1)} collective-permute-done((bf16[512,256]{1,0:T(8,128)(2,1)S(1)}, bf16[512,256]{1,0:T(8,128)(2,1)S(1)}, u32[]{:S(2)}, u32[]{:S(2)}) %collective-permute-start.1) | collective-permute-done | bytes 262176 | tf_op jit(solution)/shard_map/ppermute | solution.py:392
  34.6 1.5 %second_expand.1 = bf16[2048,256]{1,0:T(8,128)(2,1)} custom-call(s16[2048,128]{1,0:T(8,128)(2,1)S(1)} %get-tuple-element.23.cols_ref, bf16[512,256]{1,0:T(8,128)(2,1)S(1)} %collective-permute-done.1.cache_ref, bf16[2048,256]{1,0:T(8,128)(2,1)S(1)} %first_expand.1.before_ref), custom_call_target="tpu_custom_call" | custom-call | flops 536870912 | bytes 1310720 | tf_op jit(solution)/shard_map/second_expand/pallas_call | solution.py:363
  (2 shorter events, 0.0 us)
Async XLA Ops:
  0.6 1.2 %copy-start.2 = (s32[2048]{0:T(1024)S(1)}, s32[2048]{0:T(1024)}, u32[]{:S(2)}) copy-start(s32[2048]{0:T(1024)} %param.8) | copy-start | bytes 24580
  2.6 11.2 %copy-start.3 = (s32[1,8,32]{2,1,0:T(8,128)S(1)}, s32[1,8,32]{2,1,0:T(8,128)}, u32[]{:S(2)}) copy-start(s32[1,8,32]{2,1,0:T(8,128)} %param.9) | copy-start | bytes 3076
  2.6 11.3 %copy-start = (f32[2048,256]{1,0:T(8,128)S(1)}, f32[2048,256]{1,0:T(8,128)}, u32[]{:S(2)}) copy-start(f32[2048,256]{1,0:T(8,128)} %emb_ref.3) | copy-start | bytes 6291460
  2.6 11.3 %copy-start.1 = (f32[2048]{0:T(1024)S(1)}, f32[2048]{0:T(1024)}, u32[]{:S(2)}) copy-start(f32[2048]{0:T(1024)} %param.6) | copy-start | bytes 24580
  2.6 1.7 %collective-permute-start = (bf16[512,256]{1,0:T(8,128)(2,1)S(1)}, bf16[512,256]{1,0:T(8,128)(2,1)S(1)}, u32[]{:S(2)}, u32[]{:S(2)}) collective-permute-start(bf16[512,256]{1,0:T(8,128)(2,1)S(1)} %slot_sums.3), channel_id=1, source_target_pairs={{0,1},{1,0},{2,3},{3,2},{4,5},{5,4},{6,7},{7,6},{8,9},{9,8},{10,11... | collective-permute-start | bytes 786440 | tf_op jit(solution)/shard_map/ppermute | solution.py:392
  5.1 15.5 %all-to-all-start = ((bf16[16,32,256]{2,1,0:T(8,128)(2,1)}), bf16[16,32,256]{2,1,0:T(8,128)(2,1)S(1)}, u32[]{:S(2)}, u32[]{:S(2)}) async-start(bf16[16,32,256]{2,1,0:T(8,128)(2,1)} %bitcast.1), calls=%async_computation | async-start | bytes 524288 | tf_op jit(solution)/shard_map/all_to_all | solution.py:403
  21.6 11.4 %all-to-all-start.1 = ((bf16[16,32,256]{2,1,0:T(8,128)(2,1)}), bf16[16,32,256]{2,1,0:T(8,128)(2,1)S(1)}, u32[]{:S(2)}, u32[]{:S(2)}) async-start(bf16[16,32,256]{2,1,0:T(8,128)(2,1)} %get-tuple-element.17), calls=%async_computation.1 | async-start | bytes 524288 | tf_op jit(solution)/shard_map/all_to_all | solution.py:403
  33.0 1.5 %collective-permute-start.1 = (bf16[512,256]{1,0:T(8,128)(2,1)S(1)}, bf16[512,256]{1,0:T(8,128)(2,1)S(1)}, u32[]{:S(2)}, u32[]{:S(2)}) collective-permute-start(bf16[512,256]{1,0:T(8,128)(2,1)S(1)} %bitcast.6), channel_id=1, source_target_pairs={{0,1},{1,0},{2,3},{3,2},{4,5},{5,4},{6,7},{7,6},{8,9},{9,8},{10,11... | collective-permute-start | bytes 786440 | tf_op jit(solution)/shard_map/ppermute | solution.py:392
